TPU v7x, 32 devices: a whole 2x2x4 slice. The times are simulated.
32 devices in a mesh: delay: 16 (over z, y, x), row: 2 (over core).
Axes of the slice: x: 2, y: 2, z: 4, core: 2. Of those that a mesh axis runs over, the one named last changes fastest.
Arguments:
- excite: bfloat16 [1, 4096, 128], P(None, 'row'), may hold values from -6 to 6
- present_inverse: bfloat16 [32, 128, 128], P('row'), may hold values from -0.5 to 0.5
- retarded: bfloat16 [16, 32, 16, 128, 128], P('delay', 'row'), may hold values from -0.125 to 0.125
- columns: int32 [16, 32, 16], P('delay', 'row'), may hold values from 0 to 31, as said below
- future_in: float32 [16, 4096, 128], P('delay', 'row'), may hold values from -6 to 6
Outputs:
- currents: bfloat16 [1, 4096, 128], P(None, 'row')
- future_out: float32 [16, 4096, 128], P('delay', 'row')
Inputs may be any that keep to these rules, and one draw needn't show every extreme that they name: `columns`: each block row at each delay names 16 different column blocks.
All inputs are finite; a program needn't handle non-finite values.
Results may differ from a plain program's by a relative error of at most 0.0052.
Values may be sent and summed in bfloat16 or wider, within the bound.
No kernel may reach another device: no remote copies, remote signals or barrier semaphores. Data moves between devices by JAX's collectives and lax.ppermute only.
A program may use at most 64 MiB of HBM per device.

v0:
```python
import jax
import jax.numpy as jnp
from jax import lax
from jax.sharding import PartitionSpec as P

BLK = 128


def from_root(value, axis, source):
    kept = jnp.where(lax.axis_index(axis) == source, value, 0).astype(value.dtype)
    return lax.psum(kept, axis)


def from_behind(shard, axis, by):
    devices = lax.axis_size(axis)
    pairs = [(i, i + by) for i in range(devices) if 0 <= i + by < devices]
    return lax.ppermute(shard, axis, pairs)


def per_device(excite, present_inverse, retarded, columns, future_in):
    rows = future_in.shape[1]
    width = future_in.shape[2]
    row_blocks = rows // BLK
    future = future_in[0]
    weights = retarded[0]
    indices = columns[0]
    right_side = (excite[0].astype(jnp.float32) - future).astype(jnp.bfloat16)
    stacked = right_side.reshape(row_blocks, BLK, width)
    solved = lax.dot_general(
        present_inverse, stacked, (((2,), (1,)), ((0,), (0,))), preferred_element_type=jnp.float32
    )
    own_rows = solved.astype(jnp.bfloat16).reshape(rows, width)
    present = from_root(own_rows, "delay", 0)
    whole = lax.all_gather(present, "row", axis=0, tiled=True)
    history = [present]
    shifted = from_behind(future.astype(jnp.bfloat16), "delay", -1).astype(future.dtype)
    total_blocks = whole.shape[0] // BLK
    picked = whole.reshape(total_blocks, BLK, width)[indices]
    added = lax.dot_general(
        weights, picked, (((1, 3), (1, 2)), ((0,), (0,))), preferred_element_type=jnp.float32
    )
    future = shifted + added.reshape(rows, width)
    return (jnp.stack(history), future[None])


def solution(mesh):
    return jax.shard_map(
        per_device,
        mesh=mesh,
        in_specs=(
            P(None, "row", None),
            P("row", None, None),
            P("delay", "row", None, None, None),
            P("delay", "row", None),
            P("delay", "row", None),
        ),
        out_specs=(P(None, "row", None), P("delay", "row", None)),
        check_vma=False,
    )
```

profile of v0, /device:TPU:0, one launch (start us, length us, event | category | flops | bytes accessed | tf_op | source)
XLA Modules:
  0.0 161.1 jit_solution(8376958470992208895)
XLA Ops:
  7.2 0.0 copy-start
  7.2 0.0 all-reduce.2.cloned.1.call-start
  7.2 1.9 %convert_bitcast_fusion = (bf16[2048,128]{1,0:T(8,128)(2,1)S(1)}, bf16[1,2048,128]{2,1,0:T(8,128)(2,1)S(1)}) fusion(f32[1,2048,128]{2,1,0:T(8,128)} %param.9, bf16[1,2048,128]{2,1,0:T(8,128)(2,1)} %param.5), kind=kLoop, calls=%fused_computation.7 | loop fusion | flops 1048576 | bytes 2621440 | tf_op jit(solution)/shard_map/convert_element_type | solution.py:36
  9.1 0.0 copy-done
  9.1 1.1 fusion.2
  10.2 0.0 all-reduce.2.cloned.1.call-update
  10.3 0.0 all-gather.2.cloned.1.call-start
  10.3 114.5 %all-reduce.2.cloned.1.call-done = bf16[2048,128]{1,0:T(8,128)(2,1)} async-done(((bf16[2048,128]{1,0:T(8,128)(2,1)}), bf16[2048,128]{1,0:T(8,128)(2,1)}) %all-reduce.2.cloned.1.call-update) | async-done | bytes 524304 | tf_op jit(solution)/shard_map/psum | solution.py:11
  124.8 0.0 all-gather.2.cloned.1.call-update
  124.8 1.3 collective-permute-start
  126.1 0.7 compare_select_fusion
  126.8 0.1 reshape.53
  126.9 7.5 %all-gather.2.cloned.1.call-done = bf16[4096,128]{1,0:T(8,128)(2,1)} async-done(((bf16[2048,128]{1,0:T(8,128)(2,1)}), bf16[4096,128]{1,0:T(8,128)(2,1)}) %all-gather.2.cloned.1.call-update) | async-done | bytes 1048592 | tf_op jit(solution)/shard_map/all_gather | solution.py:34
  134.4 9.8 %gather_fusion = bf16[256,128,128]{2,1,0:T(8,128)(2,1)} fusion(bf16[32,128,128]{2,1,0:T(8,128)(2,1)} %bitcast.27, s32[1024]{0:T(1024)S(1)} %pad_clamp_fusion), kind=kCustom, calls=%fused_computation | custom fusion | bytes 16778240 | tf_op jit(solution)/shard_map/gather | solution.py:38
  144.2 0.0 copy-start.1
  144.2 8.2 %fusion = f32[16,128,128,1]{1,2,3,0:T(8,128)S(1)} fusion(bf16[16,16,128,128]{3,2,1,0:T(8,128)(2,1)} %bitcast.28, bf16[1,16,16,128,128]{4,3,2,1,0:T(8,128)(2,1)} %param.7), kind=kOutput, calls=%fused_computation.1 | convolution fusion | flops 1073741824 | bytes 17825792 | tf_op jit(solution)/shard_map/dot_general | solution.py:39
  152.4 0.0 collective-permute-done
  152.4 1.1 bitcast_add_fusion
  153.5 0.0 copy-done.1
  153.5 0.8 copy.9
  (1 shorter events, 0.0 us)
Async XLA Ops:
  7.2 2.0 %copy-start = (bf16[16,128,128]{2,1,0:T(8,128)(2,1)S(1)}, bf16[16,128,128]{2,1,0:T(8,128)(2,1)}, u32[]{:S(2)}) copy-start(bf16[16,128,128]{2,1,0:T(8,128)(2,1)} %param.6) | copy-start | bytes 1572868
  7.2 117.6 %all-reduce.2.cloned.1.call-start = ((), (), s32[]{:S(2)}) async-start(), calls=%async_computation | async-start | bytes 1048576 | tf_op jit(solution)/shard_map/psum | solution.py:11
  10.3 124.1 %all-gather.2.cloned.1.call-start = ((), (), s32[]{:S(2)}) async-start(), calls=%async_computation.1 | async-start | bytes 1572864 | tf_op jit(solution)/shard_map/all_gather | solution.py:34
  124.8 27.6 %collective-permute-start = (bf16[2048,128]{1,0:T(8,128)(2,1)S(1)}, bf16[2048,128]{1,0:T(8,128)(2,1)S(1)}, u32[]{:S(2)}, u32[]{:S(2)}) collective-permute-start(bf16[2048,128]{1,0:T(8,128)(2,1)S(1)} %get-tuple-element.2), channel_id=1, source_target_pairs={{2,0},{4,2},{6,4},{8,6},{10,8},{12,10},{14,12},{16,14},{18,16},{20... | collective-permute-start | bytes 1572872 | tf_op jit(solution)/shard_map/ppermute | solution.py:17
  144.2 9.2 %copy-start.1 = (bf16[2048,128]{1,0:T(8,128)(2,1)S(1)}, bf16[2048,128]{1,0:T(8,128)(2,1)}, u32[]{:S(2)}) copy-start(bf16[2048,128]{1,0:T(8,128)(2,1)} %all-reduce.2.cloned.1.call-done) | copy-start | bytes 1572868
Sparse Core Ops, SparseCore 0:
  13.7 111.0 all-reduce.1
  126.4 7.9 all-gather.1
where the time goes:
time: 161 us
  waiting for transfers between devices  122 us (76%)
  between operations  14.1 us (9%)
  local copies, waits for them, and re-layouts  10.7 us (7%)
  matrix products  9.25 us (6%)
  other arithmetic  3.66 us (2%)
    psum x1, waiting for transfers between devices, from_root(): return lax.psum(kept, axis)  114 us
    gather x1, local copies, waits for them, and re-layouts, per_device(): picked = whole.reshape(total_blocks, BLK, width)[indices]  9.85 us
    dot_general x1, matrix products, per_device(): lax.dot_general(weights, picked, (((1, 3), (1, 2)), ((0,), (0,))), prefer...  8.16 us
    all_gather x1, waiting for transfers between devices, per_device(): whole = lax.all_gather(present, 'row', axis=0, tiled=True)  7.51 us
  transfers between devices with their start and end apart: 3, of which 2 were waited for; matrix products, arithmetic and copies ran while one was open for 12% of the time, Pallas kernels for 0%

commit v1 on v0

v1 whole, which is shorter than its diff:
```python
import functools

import jax
import jax.numpy as jnp
from jax import lax
from jax.experimental import pallas as pl
from jax.experimental.pallas import tpu as pltpu
from jax.sharding import PartitionSpec as P

BLK = 128
PLANE = 4

VMEM_SPEC = pl.BlockSpec(memory_space=pltpu.VMEM)
ANY_SPEC = pl.BlockSpec(memory_space=pl.ANY)
SMEM_SPEC = pl.BlockSpec(memory_space=pltpu.SMEM)


def solve_kernel(excite_hbm, inverse_hbm, future_hbm, *refs):
    quarters = refs[:PLANE]
    excite, inverse, future, sems = refs[PLANE:]
    step = quarters[0].shape[0]
    blocks = step // BLK
    root = lax.axis_index("delay") == 0

    def copies(part):
        rows = pl.ds(part * step, step)
        whole = pl.ds(part * blocks, blocks)
        return (
            pltpu.make_async_copy(future_hbm.at[0, rows], future.at[rows], sems.at[0, part]),
            pltpu.make_async_copy(excite_hbm.at[0, rows], excite.at[rows], sems.at[1, part]),
            pltpu.make_async_copy(inverse_hbm.at[whole], inverse.at[whole], sems.at[2, part]),
        )

    @pl.when(root)
    def _():
        for part in reversed(range(PLANE)):
            for copy in copies(part):
                copy.start()
        for part in reversed(range(PLANE)):
            for copy in copies(part):
                copy.wait()
            for block in range(blocks):
                rows = pl.ds(part * step + block * BLK, BLK)
                right = (excite[rows, :].astype(jnp.float32) - future[rows, :]).astype(jnp.bfloat16)
                solved = jnp.dot(
                    inverse[part * blocks + block], right, preferred_element_type=jnp.float32
                )
                quarters[part][pl.ds(block * BLK, BLK), :] = solved.astype(jnp.bfloat16)

    @pl.when(jnp.logical_not(root))
    def _():
        quarters[0][...] = jnp.zeros_like(quarters[0])


def solve(excite, inverse, future):
    rows, width = future.shape[1:]
    quarter = jax.ShapeDtypeStruct((rows // PLANE, width), jnp.bfloat16)
    return pl.pallas_call(
        solve_kernel,
        out_shape=[quarter] * PLANE,
        in_specs=[ANY_SPEC] * 3,
        out_specs=[VMEM_SPEC] * PLANE,
        scratch_shapes=[
            pltpu.VMEM((rows, width), jnp.bfloat16),
            pltpu.VMEM(inverse.shape, jnp.bfloat16),
            pltpu.VMEM((rows, width), jnp.float32),
            pltpu.SemaphoreType.DMA((3, PLANE)),
        ],
    )(excite, inverse, future)


def narrow_kernel(future, out):
    out[...] = future[0].astype(jnp.bfloat16)


def narrow(future):
    rows, width = future.shape[1:]
    return pl.pallas_call(
        narrow_kernel,
        out_shape=jax.ShapeDtypeStruct((rows, width), jnp.bfloat16),
        in_specs=[VMEM_SPEC],
        out_specs=VMEM_SPEC,
    )(future)


def fetch_kernel(weights_hbm, out, sem):
    copy = pltpu.make_async_copy(weights_hbm.at[0], out, sem)
    copy.start()
    copy.wait()


def fetch(weights):
    return pl.pallas_call(
        fetch_kernel,
        out_shape=jax.ShapeDtypeStruct(weights.shape[1:], weights.dtype),
        in_specs=[ANY_SPEC],
        out_specs=VMEM_SPEC,
        scratch_shapes=[pltpu.SemaphoreType.DMA],
        compiler_params=pltpu.CompilerParams(vmem_limit_bytes=40 << 20),
    )(weights)


def product_kernel(halves, columns, weights, shifted, *refs):
    pieces = refs[: halves * PLANE]
    currents_hbm, future_hbm, whole, total, sems = refs[halves * PLANE :]
    step = pieces[0].shape[0] // BLK
    row_blocks, slots = weights.shape[:2]
    mine = lax.rem(lax.axis_index("delay"), PLANE)
    row = lax.axis_index("row")
    for turn in range(halves):
        half = lax.rem(row - turn + halves, halves)
        for mask in range(PLANE):
            start = (half * PLANE + lax.bitwise_xor(mine, mask)) * step
            piece = pieces[turn * PLANE + mask]
            for block in range(step):
                whole[start + block] = piece[pl.ds(block * BLK, BLK), :]

    own = pltpu.make_async_copy(
        whole.at[pl.ds(row * row_blocks, row_blocks)], currents_hbm, sems.at[row_blocks]
    )
    own.start()

    def out_copy(r):
        rows = pl.ds(r * BLK, BLK)
        return pltpu.make_async_copy(total.at[rows], future_hbm.at[rows], sems.at[r])

    def one_row(r, carry):
        left = jnp.concatenate([weights[r, k] for k in range(slots)], axis=1)
        right = jnp.concatenate([whole[columns[0, r, k]] for k in range(slots)], axis=0)
        rows = pl.ds(pl.multiple_of(r * BLK, BLK), BLK)
        added = jnp.dot(left, right, preferred_element_type=jnp.float32)
        total[rows, :] = shifted[rows, :].astype(jnp.float32) + added
        out_copy(r).start()
        return carry

    lax.fori_loop(0, row_blocks, one_row, 0)
    own.wait()

    def one_wait(r, carry):
        out_copy(r).wait()
        return carry

    lax.fori_loop(0, row_blocks, one_wait, 0)


def product(columns, weights, shifted, pieces, halves):
    row_blocks = weights.shape[0]
    rows, width = shifted.shape
    return pl.pallas_call(
        functools.partial(product_kernel, halves),
        out_shape=[
            jax.ShapeDtypeStruct((row_blocks, BLK, width), jnp.bfloat16),
            jax.ShapeDtypeStruct((rows, width), jnp.float32),
        ],
        in_specs=[SMEM_SPEC, VMEM_SPEC, VMEM_SPEC] + [VMEM_SPEC] * len(pieces),
        out_specs=[ANY_SPEC, ANY_SPEC],
        scratch_shapes=[
            pltpu.VMEM((halves * row_blocks, BLK, width), jnp.bfloat16),
            pltpu.VMEM((rows, width), jnp.float32),
            pltpu.SemaphoreType.DMA((row_blocks + 1,)),
        ],
        compiler_params=pltpu.CompilerParams(vmem_limit_bytes=40 << 20),
    )(columns, weights, shifted, *pieces)


def per_device(excite, present_inverse, retarded, columns, future_in):
    delays, halves = lax.axis_size("delay"), lax.axis_size("row")
    planes = delays // PLANE
    rows, width = future_in.shape[1:]

    quarters = solve(excite, present_inverse, future_in)
    spread = [lax.ppermute(quarters[k], "delay", [(0, k)]) for k in (3, 2, 1)]
    weights, narrowed = fetch(retarded), narrow(future_in)
    spread, weights, narrowed = lax.optimization_barrier((spread, weights, narrowed))
    shifted = lax.ppermute(narrowed, "delay", [(i, i - 1) for i in range(1, delays)])
    piece = quarters[0] + spread[0] + spread[1] + spread[2]
    reach = planes
    while reach > 1:
        reach //= 2
        pairs = [
            (z * PLANE + q, (z + reach) * PLANE + q)
            for z in range(0, planes, 2 * reach)
            for q in range(PLANE)
        ]
        piece = piece + lax.ppermute(piece, "delay", pairs)
    held = [piece] + [None] * (PLANE - 1)
    for mask in (3, 1, 2):
        held[mask] = lax.ppermute(piece, "delay", [(i, i ^ mask) for i in range(delays)])
    pieces = list(held)
    for turn in range(1, halves):
        pairs = [(i, (i + turn) % halves) for i in range(halves)]
        pieces += [lax.ppermute(p, "row", pairs) for p in held]
    currents, future = product(columns, weights, shifted, pieces, halves)
    return currents.reshape(1, rows, width), future[None]


def solution(mesh):
    return jax.shard_map(
        per_device,
        mesh=mesh,
        in_specs=(
            P(None, "row", None),
            P("row", None, None),
            P("delay", "row", None, None, None),
            P("delay", "row", None),
            P("delay", "row", None),
        ),
        out_specs=(P(None, "row", None), P("delay", "row", None)),
        check_vma=False,
    )
```

time: 161 us -> 45.7 us (0.28)
  waiting for transfers between devices: 122 us -> 13.5 us
  starting transfers between devices: 1.37 us -> 16.6 us
  Pallas kernels: 0 us -> 14.4 us
  between operations: 14.1 us -> 0.77 us
  local copies, waits for them, and re-layouts: 10.7 us -> 0.01 us
  matrix products: 9.25 us -> 0 us
  other arithmetic: 3.66 us -> 0.11 us
    psum x1 -> x0, waiting for transfers between devices: 114 us -> none  [from_root(): return lax.psum(kept, axis)]
    ppermute x1 -> x13, starting transfers between devices: 1.29 us -> 16.6 us  [the longest x3 6.65 us: per_device(): spread = [lax.ppermute(quarters[k], 'delay', [(0, k)]) for k in (3, 2, 1)]]
    pallas_call x0 -> x4, Pallas kernels: none -> 14.4 us  [the longest x1 6.24 us: product(): pl.pallas_call(functools.partial(product_kernel, halves), out_shape=[jax....]
    ppermute x1 -> x13, waiting for transfers between devices: 0.01 us -> 13.5 us  [the longest x3 8.23 us: per_device(): lax.ppermute(piece, 'delay', [(i, i ^ mask) for i in range(delays)])]
    gather x1 -> x0, local copies, waits for them, and re-layouts: 9.85 us -> none  [per_device(): picked = whole.reshape(total_blocks, BLK, width)[indices]]
    dot_general x2 -> x0, matrix products: 9.25 us -> none  [the longest x1 8.16 us: per_device(): lax.dot_general(weights, picked, (((1, 3), (1, 2)), ((0,), (0,))), prefer...]
    all_gather x1 -> x0, waiting for transfers between devices: 7.51 us -> none  [per_device(): whole = lax.all_gather(present, 'row', axis=0, tiled=True)]
    convert_element_type x1 -> x0, other arithmetic: 1.89 us -> none  [per_device(): future.astype(jnp.bfloat16)]
  transfers between devices with their start and end apart: 3 -> 13, of which waited for: 2 -> 5; matrix products, arithmetic and copies ran while one was open for 12% -> 0% of each run, Pallas kernels for 0% -> 12%
where the time goes in v1:
time: 45.7 us; the launch traced here: 45.4 us
  starting transfers between devices  16.6 us (36%)
  Pallas kernels  14.4 us (32%)
  waiting for transfers between devices  13.5 us (30%)
  between operations  0.77 us (2%)
    ppermute x3, waiting for transfers between devices, per_device(): lax.ppermute(piece, 'delay', [(i, i ^ mask) for i in range(delays)])  8.23 us
    ppermute x3, starting transfers between devices, per_device(): spread = [lax.ppermute(quarters[k], 'delay', [(0, k)]) for k in (3, 2, 1)]  6.65 us
    pallas_call x1, Pallas kernels, product(): pl.pallas_call(functools.partial(product_kernel, halves), out_shape=[jax....  6.24 us
    ppermute x2, starting transfers between devices, per_device(): piece = piece + lax.ppermute(piece, 'delay', pairs)  4.59 us
    ppermute x2, waiting for transfers between devices, per_device(): piece = piece + lax.ppermute(piece, 'delay', pairs)  3.92 us
    ppermute x3, starting transfers between devices, per_device(): lax.ppermute(piece, 'delay', [(i, i ^ mask) for i in range(delays)])  3.55 us
    pallas_call x1, Pallas kernels, fetch(): pl.pallas_call(fetch_kernel, out_shape=jax.ShapeDtypeStruct(weights.shape...  3.45 us
    pallas_call x1, Pallas kernels, solve(): pl.pallas_call(solve_kernel, out_shape=[quarter] * PLANE, in_specs=[ANY_S...  2.68 us
  transfers between devices with their start and end apart: 13, of which 5 were waited for; matrix products, arithmetic and copies ran while one was open for 0% of the time, Pallas kernels for 12%

profile of v1, /device:TPU:0, one launch (start us, length us, event | category | flops | bytes accessed | tf_op | source)
XLA Modules:
  0.0 45.4 jit_solution(6258085142358878050)
XLA Ops:
  0.6 2.7 %shard_map.68 = (bf16[512,128]{1,0:T(8,128)(2,1)}, bf16[512,128]{1,0:T(8,128)(2,1)}, bf16[512,128]{1,0:T(8,128)(2,1)}, bf16[512,128]{1,0:T(8,128)(2,1)}) custom-call(bf16[1,2048,128]{2,1,0:T(8,128)(2,1)} %excite_hbm.1, bf16[16,128,128]{2,1,0:T(8,128)(2,1)} %inverse_hbm.1, f32[1,2048,128]{2,1,0:T(8,128)} %future.1), custom_call_target="tpu_custom_call" | custom-call | tf_op jit(solution)/shard_map/pallas_call | solution.py:58
  3.3 4.1 %collective-permute-start = (bf16[512,128]{1,0:T(8,128)(2,1)}, bf16[512,128]{1,0:T(8,128)(2,1)S(1)}, u32[]{:S(2)}, u32[]{:S(2)}) collective-permute-start(bf16[512,128]{1,0:T(8,128)(2,1)} %get-tuple-element.13), channel_id=1, source_target_pairs={{0,6},{1,7}} | collective-permute-start | bytes 393224 | tf_op jit(solution)/shard_map/ppermute | solution.py:172
  7.4 1.3 %collective-permute-start.1 = (bf16[512,128]{1,0:T(8,128)(2,1)}, bf16[512,128]{1,0:T(8,128)(2,1)S(1)}, u32[]{:S(2)}, u32[]{:S(2)}) collective-permute-start(bf16[512,128]{1,0:T(8,128)(2,1)} %get-tuple-element.14), channel_id=1, source_target_pairs={{0,4},{1,5}} | collective-permute-start | bytes 393224 | tf_op jit(solution)/shard_map/ppermute | solution.py:172
  8.7 1.3 %collective-permute-start.2 = (bf16[512,128]{1,0:T(8,128)(2,1)}, bf16[512,128]{1,0:T(8,128)(2,1)S(1)}, u32[]{:S(2)}, u32[]{:S(2)}) collective-permute-start(bf16[512,128]{1,0:T(8,128)(2,1)} %get-tuple-element.15), channel_id=1, source_target_pairs={{0,2},{1,3}} | collective-permute-start | bytes 393224 | tf_op jit(solution)/shard_map/ppermute | solution.py:172
  10.0 2.1 %shard_map.70 = bf16[2048,128]{1,0:T(8,128)(2,1)} custom-call(f32[1,2048,128]{2,1,0:T(8,128)} %future.1), custom_call_target="tpu_custom_call" | custom-call | tf_op jit(solution)/shard_map/pallas_call | solution.py:78
  12.1 3.5 %shard_map.69.weights = bf16[16,16,128,128]{3,2,1,0:T(8,128)(2,1)S(1)} custom-call(bf16[1,16,16,128,128]{4,3,2,1,0:T(8,128)(2,1)} %weights_hbm.1), custom_call_target="tpu_custom_call" | custom-call | tf_op jit(solution)/shard_map/pallas_call | solution.py:93
  15.5 0.0 collective-permute-done
  15.5 0.0 collective-permute-done.1
  15.6 1.3 %collective-permute-start.4 = (bf16[512,128]{1,0:T(8,128)(2,1)S(1)}, bf16[512,128]{1,0:T(8,128)(2,1)S(1)}, u32[]{:S(2)}, u32[]{:S(2)}) collective-permute-start(bf16[512,128]{1,0:T(8,128)(2,1)S(1)} %add_add_fusion), channel_id=1, source_target_pairs={{0,16},{2,18},{4,20},{6,22},{1,17},{3,19},{5,21},{7,23}} | collective-permute-start | bytes 393224 | tf_op jit(solution)/shard_map/ppermute | solution.py:185
  16.9 1.3 %collective-permute-start.3 = (bf16[2048,128]{1,0:T(8,128)(2,1)S(1)}, bf16[2048,128]{1,0:T(8,128)(2,1)S(1)}, u32[]{:S(2)}, u32[]{:S(2)}) collective-permute-start(bf16[2048,128]{1,0:T(8,128)(2,1)S(1)} %copy-done.1), channel_id=1, source_target_pairs={{2,0},{4,2},{6,4},{8,6},{10,8},{12,10},{14,12},{16,14},{18,16},{20... | collective-permute-start | bytes 1572872 | tf_op jit(solution)/shard_map/ppermute | solution.py:175
  18.2 1.4 %collective-permute-done.4 = bf16[512,128]{1,0:T(8,128)(2,1)S(1)} collective-permute-done((bf16[512,128]{1,0:T(8,128)(2,1)S(1)}, bf16[512,128]{1,0:T(8,128)(2,1)S(1)}, u32[]{:S(2)}, u32[]{:S(2)}) %collective-permute-start.4) | collective-permute-done | bytes 131104 | tf_op jit(solution)/shard_map/ppermute | solution.py:185
  19.7 3.3 %collective-permute-start.5 = (bf16[512,128]{1,0:T(8,128)(2,1)S(1)}, bf16[512,128]{1,0:T(8,128)(2,1)S(1)}, u32[]{:S(2)}, u32[]{:S(2)}) collective-permute-start(bf16[512,128]{1,0:T(8,128)(2,1)S(1)} %add.18), channel_id=1, source_target_pairs={{0,8},{2,10},{4,12},{6,14},{16,24},{18,26},{20,28},{22,30},{1,9},{... | collective-permute-start | bytes 393224 | tf_op jit(solution)/shard_map/ppermute | solution.py:185
  23.0 2.5 %collective-permute-done.5 = bf16[512,128]{1,0:T(8,128)(2,1)S(1)} collective-permute-done((bf16[512,128]{1,0:T(8,128)(2,1)S(1)}, bf16[512,128]{1,0:T(8,128)(2,1)S(1)}, u32[]{:S(2)}, u32[]{:S(2)}) %collective-permute-start.5) | collective-permute-done | bytes 131104 | tf_op jit(solution)/shard_map/ppermute | solution.py:185
  25.5 0.1 collective-permute-start.8
  25.6 0.7 %collective-permute-start.7 = (bf16[512,128]{1,0:T(8,128)(2,1)S(1)}, bf16[512,128]{1,0:T(8,128)(2,1)S(1)}, u32[]{:S(2)}, u32[]{:S(2)}) collective-permute-start(bf16[512,128]{1,0:T(8,128)(2,1)S(1)} %add.19.refs_0_), channel_id=1, source_target_pairs={{0,4},{2,6},{4,0},{6,2},{8,12},{10,14},{12,8},{14,10},{16,20},{18,... | collective-permute-start | bytes 393224 | tf_op jit(solution)/shard_map/ppermute | solution.py:188
  26.3 2.8 %collective-permute-start.6 = (bf16[512,128]{1,0:T(8,128)(2,1)S(1)}, bf16[512,128]{1,0:T(8,128)(2,1)S(1)}, u32[]{:S(2)}, u32[]{:S(2)}) collective-permute-start(bf16[512,128]{1,0:T(8,128)(2,1)S(1)} %add.19.refs_0_), channel_id=1, source_target_pairs={{0,2},{2,0},{4,6},{6,4},{8,10},{10,8},{12,14},{14,12},{16,18},{18,... | collective-permute-start | bytes 393224 | tf_op jit(solution)/shard_map/ppermute | solution.py:188
  29.1 6.5 %collective-permute-done.8.refs_3_ = bf16[512,128]{1,0:T(8,128)(2,1)S(1)} collective-permute-done((bf16[512,128]{1,0:T(8,128)(2,1)S(1)}, bf16[512,128]{1,0:T(8,128)(2,1)S(1)}, u32[]{:S(2)}, u32[]{:S(2)}) %collective-permute-start.8) | collective-permute-done | bytes 131104 | tf_op jit(solution)/shard_map/ppermute | solution.py:188
  35.6 0.0 collective-permute-done.7.refs_2_
  35.6 0.5 %collective-permute-start.11 = (bf16[512,128]{1,0:T(8,128)(2,1)S(1)}, bf16[512,128]{1,0:T(8,128)(2,1)S(1)}, u32[]{:S(2)}, u32[]{:S(2)}) collective-permute-start(bf16[512,128]{1,0:T(8,128)(2,1)S(1)} %collective-permute-done.7.refs_2_), channel_id=1, source_target_pairs={{0,1},{1,0},{2,3},{3,2},{4,5},{5,4},{6,7},{7,6},{8,9},{9,8},{10,11... | collective-permute-start | bytes 393224 | tf_op jit(solution)/shard_map/ppermute | solution.py:192
  36.1 1.7 %collective-permute-done.6.refs_1_ = bf16[512,128]{1,0:T(8,128)(2,1)S(1)} collective-permute-done((bf16[512,128]{1,0:T(8,128)(2,1)S(1)}, bf16[512,128]{1,0:T(8,128)(2,1)S(1)}, u32[]{:S(2)}, u32[]{:S(2)}) %collective-permute-start.6) | collective-permute-done | bytes 131104 | tf_op jit(solution)/shard_map/ppermute | solution.py:188
  37.8 0.0 collective-permute-done.9.refs_4_
  37.8 0.0 collective-permute-done.12.refs_7_
  37.8 1.3 %collective-permute-done.10.refs_5_ = bf16[512,128]{1,0:T(8,128)(2,1)S(1)} collective-permute-done((bf16[512,128]{1,0:T(8,128)(2,1)S(1)}, bf16[512,128]{1,0:T(8,128)(2,1)S(1)}, u32[]{:S(2)}, u32[]{:S(2)}) %collective-permute-start.10) | collective-permute-done | bytes 131104 | tf_op jit(solution)/shard_map/ppermute | solution.py:192
  39.2 6.2 %shard_map.71 = (bf16[16,128,128]{2,1,0:T(8,128)(2,1)}, f32[2048,128]{1,0:T(8,128)}) custom-call(s32[1,16,16]{2,1,0:T(8,128)S(1)} %copy-done, bf16[16,16,128,128]{3,2,1,0:T(8,128)(2,1)S(1)} %shard_map.69.weights, bf16[2048,128]{1,0:T(8,128)(2,1)S(1)} %collective-permute-done.3.shifted, bf16[512,128]{1,0:T(8,128)(2,1)S(1)} %add.19.refs_0_, ...), custom_call_target="tpu_custom_call" | custom-call | tf_op jit(solution)/shard_map/pallas_call | solution.py:149
  (15 shorter events, 0.1 us)
Async XLA Ops:
  3.3 12.2 %collective-permute-start = (bf16[512,128]{1,0:T(8,128)(2,1)}, bf16[512,128]{1,0:T(8,128)(2,1)S(1)}, u32[]{:S(2)}, u32[]{:S(2)}) collective-permute-start(bf16[512,128]{1,0:T(8,128)(2,1)} %get-tuple-element.13), channel_id=1, source_target_pairs={{0,6},{1,7}} | collective-permute-start | bytes 393224 | tf_op jit(solution)/shard_map/ppermute | solution.py:172
  7.4 8.2 %collective-permute-start.1 = (bf16[512,128]{1,0:T(8,128)(2,1)}, bf16[512,128]{1,0:T(8,128)(2,1)S(1)}, u32[]{:S(2)}, u32[]{:S(2)}) collective-permute-start(bf16[512,128]{1,0:T(8,128)(2,1)} %get-tuple-element.14), channel_id=1, source_target_pairs={{0,4},{1,5}} | collective-permute-start | bytes 393224 | tf_op jit(solution)/shard_map/ppermute | solution.py:172
  8.7 6.9 %collective-permute-start.2 = (bf16[512,128]{1,0:T(8,128)(2,1)}, bf16[512,128]{1,0:T(8,128)(2,1)S(1)}, u32[]{:S(2)}, u32[]{:S(2)}) collective-permute-start(bf16[512,128]{1,0:T(8,128)(2,1)} %get-tuple-element.15), channel_id=1, source_target_pairs={{0,2},{1,3}} | collective-permute-start | bytes 393224 | tf_op jit(solution)/shard_map/ppermute | solution.py:172
  12.1 3.5 %copy-start.2 = (bf16[512,128]{1,0:T(8,128)(2,1)S(1)}, bf16[512,128]{1,0:T(8,128)(2,1)}, u32[]{:S(2)}) copy-start(bf16[512,128]{1,0:T(8,128)(2,1)} %get-tuple-element.18) | copy-start | bytes 393220
  12.1 4.9 %copy-start.1 = (bf16[2048,128]{1,0:T(8,128)(2,1)S(1)}, bf16[2048,128]{1,0:T(8,128)(2,1)}, u32[]{:S(2)}) copy-start(bf16[2048,128]{1,0:T(8,128)(2,1)} %shard_map.70) | copy-start | bytes 1572868
  12.1 27.1 %copy-start = (s32[1,16,16]{2,1,0:T(8,128)S(1)}, s32[1,16,16]{2,1,0:T(8,128)}, u32[]{:S(2)}) copy-start(s32[1,16,16]{2,1,0:T(8,128)} %columns.1) | copy-start | bytes 3076
  15.6 4.0 %collective-permute-start.4 = (bf16[512,128]{1,0:T(8,128)(2,1)S(1)}, bf16[512,128]{1,0:T(8,128)(2,1)S(1)}, u32[]{:S(2)}, u32[]{:S(2)}) collective-permute-start(bf16[512,128]{1,0:T(8,128)(2,1)S(1)} %add_add_fusion), channel_id=1, source_target_pairs={{0,16},{2,18},{4,20},{6,22},{1,17},{3,19},{5,21},{7,23}} | collective-permute-start | bytes 393224 | tf_op jit(solution)/shard_map/ppermute | solution.py:185
  16.9 22.2 %collective-permute-start.3 = (bf16[2048,128]{1,0:T(8,128)(2,1)S(1)}, bf16[2048,128]{1,0:T(8,128)(2,1)S(1)}, u32[]{:S(2)}, u32[]{:S(2)}) collective-permute-start(bf16[2048,128]{1,0:T(8,128)(2,1)S(1)} %copy-done.1), channel_id=1, source_target_pairs={{2,0},{4,2},{6,4},{8,6},{10,8},{12,10},{14,12},{16,14},{18,16},{20... | collective-permute-start | bytes 1572872 | tf_op jit(solution)/shard_map/ppermute | solution.py:175
  19.7 5.8 %collective-permute-start.5 = (bf16[512,128]{1,0:T(8,128)(2,1)S(1)}, bf16[512,128]{1,0:T(8,128)(2,1)S(1)}, u32[]{:S(2)}, u32[]{:S(2)}) collective-permute-start(bf16[512,128]{1,0:T(8,128)(2,1)S(1)} %add.18), channel_id=1, source_target_pairs={{0,8},{2,10},{4,12},{6,14},{16,24},{18,26},{20,28},{22,30},{1,9},{... | collective-permute-start | bytes 393224 | tf_op jit(solution)/shard_map/ppermute | solution.py:185
  25.5 10.1 %collective-permute-start.8 = (bf16[512,128]{1,0:T(8,128)(2,1)S(1)}, bf16[512,128]{1,0:T(8,128)(2,1)S(1)}, u32[]{:S(2)}, u32[]{:S(2)}) collective-permute-start(bf16[512,128]{1,0:T(8,128)(2,1)S(1)} %add.19.refs_0_), channel_id=1, source_target_pairs={{0,6},{2,4},{4,2},{6,0},{8,14},{10,12},{12,10},{14,8},{16,22},{18,... | collective-permute-start | bytes 393224 | tf_op jit(solution)/shard_map/ppermute | solution.py:188
  25.6 10.0 %collective-permute-start.7 = (bf16[512,128]{1,0:T(8,128)(2,1)S(1)}, bf16[512,128]{1,0:T(8,128)(2,1)S(1)}, u32[]{:S(2)}, u32[]{:S(2)}) collective-permute-start(bf16[512,128]{1,0:T(8,128)(2,1)S(1)} %add.19.refs_0_), channel_id=1, source_target_pairs={{0,4},{2,6},{4,0},{6,2},{8,12},{10,14},{12,8},{14,10},{16,20},{18,... | collective-permute-start | bytes 393224 | tf_op jit(solution)/shard_map/ppermute | solution.py:188
  26.3 11.5 %collective-permute-start.6 = (bf16[512,128]{1,0:T(8,128)(2,1)S(1)}, bf16[512,128]{1,0:T(8,128)(2,1)S(1)}, u32[]{:S(2)}, u32[]{:S(2)}) collective-permute-start(bf16[512,128]{1,0:T(8,128)(2,1)S(1)} %add.19.refs_0_), channel_id=1, source_target_pairs={{0,2},{2,0},{4,6},{6,4},{8,10},{10,8},{12,14},{14,12},{16,18},{18,... | collective-permute-start | bytes 393224 | tf_op jit(solution)/shard_map/ppermute | solution.py:188
  29.1 8.7 %collective-permute-start.9 = (bf16[512,128]{1,0:T(8,128)(2,1)S(1)}, bf16[512,128]{1,0:T(8,128)(2,1)S(1)}, u32[]{:S(2)}, u32[]{:S(2)}) collective-permute-start(bf16[512,128]{1,0:T(8,128)(2,1)S(1)} %add.19.refs_0_), channel_id=1, source_target_pairs={{0,1},{1,0},{2,3},{3,2},{4,5},{5,4},{6,7},{7,6},{8,9},{9,8},{10,11... | collective-permute-start | bytes 393224 | tf_op jit(solution)/shard_map/ppermute | solution.py:192
  35.6 2.2 %collective-permute-start.12 = (bf16[512,128]{1,0:T(8,128)(2,1)S(1)}, bf16[512,128]{1,0:T(8,128)(2,1)S(1)}, u32[]{:S(2)}, u32[]{:S(2)}) collective-permute-start(bf16[512,128]{1,0:T(8,128)(2,1)S(1)} %collective-permute-done.8.refs_3_), channel_id=1, source_target_pairs={{0,1},{1,0},{2,3},{3,2},{4,5},{5,4},{6,7},{7,6},{8,9},{9,8},{10,11... | collective-permute-start | bytes 393224 | tf_op jit(solution)/shard_map/ppermute | solution.py:192
  35.6 2.2 %collective-permute-start.11 = (bf16[512,128]{1,0:T(8,128)(2,1)S(1)}, bf16[512,128]{1,0:T(8,128)(2,1)S(1)}, u32[]{:S(2)}, u32[]{:S(2)}) collective-permute-start(bf16[512,128]{1,0:T(8,128)(2,1)S(1)} %collective-permute-done.7.refs_2_), channel_id=1, source_target_pairs={{0,1},{1,0},{2,3},{3,2},{4,5},{5,4},{6,7},{7,6},{8,9},{9,8},{10,11... | collective-permute-start | bytes 393224 | tf_op jit(solution)/shard_map/ppermute | solution.py:192
  37.8 1.3 %collective-permute-start.10 = (bf16[512,128]{1,0:T(8,128)(2,1)S(1)}, bf16[512,128]{1,0:T(8,128)(2,1)S(1)}, u32[]{:S(2)}, u32[]{:S(2)}) collective-permute-start(bf16[512,128]{1,0:T(8,128)(2,1)S(1)} %collective-permute-done.6.refs_1_), channel_id=1, source_target_pairs={{0,1},{1,0},{2,3},{3,2},{4,5},{5,4},{6,7},{7,6},{8,9},{9,8},{10,11... | collective-permute-start | bytes 393224 | tf_op jit(solution)/shard_map/ppermute | solution.py:192

commit v2 on v1

--- a/solution.py
+++ b/solution.py
@@ -54,7 +54,7 @@
 
 def solve(excite, inverse, future):
     rows, width = future.shape[1:]
-    quarter = jax.ShapeDtypeStruct((rows // PLANE, width), jnp.bfloat16)
+    quarter = pltpu.VMEM((rows // PLANE, width), jnp.bfloat16)
     return pl.pallas_call(
         solve_kernel,
         out_shape=[quarter] * PLANE,
@@ -69,42 +69,58 @@
     )(excite, inverse, future)
 
 
-def narrow_kernel(future, out):
-    out[...] = future[0].astype(jnp.bfloat16)
+def narrow_kernel(parts, future_hbm, out, future, sems):
+    step = future.shape[0] // parts
+
+    def copy(part):
+        rows = pl.ds(part * step, step)
+        return pltpu.make_async_copy(future_hbm.at[0, rows], future.at[rows], sems.at[part])
+
+    for part in range(parts):
+        copy(part).start()
+    for part in range(parts):
+        copy(part).wait()
+        rows = pl.ds(part * step, step)
+        out[rows, :] = future[rows, :].astype(jnp.bfloat16)
 
 
 def narrow(future):
     rows, width = future.shape[1:]
     return pl.pallas_call(
-        narrow_kernel,
-        out_shape=jax.ShapeDtypeStruct((rows, width), jnp.bfloat16),
-        in_specs=[VMEM_SPEC],
+        functools.partial(narrow_kernel, PLANE),
+        out_shape=pltpu.VMEM((rows, width), jnp.bfloat16),
+        in_specs=[ANY_SPEC],
         out_specs=VMEM_SPEC,
+        scratch_shapes=[
+            pltpu.VMEM((rows, width), jnp.float32),
+            pltpu.SemaphoreType.DMA((PLANE,)),
+        ],
     )(future)
 
 
-def fetch_kernel(weights_hbm, out, sem):
-    copy = pltpu.make_async_copy(weights_hbm.at[0], out, sem)
+def fetch_kernel(first, weights_hbm, out, sem):
+    copy = pltpu.make_async_copy(weights_hbm.at[0, pl.ds(first, out.shape[0])], out, sem)
     copy.start()
     copy.wait()
 
 
-def fetch(weights):
-    return pl.pallas_call(
-        fetch_kernel,
-        out_shape=jax.ShapeDtypeStruct(weights.shape[1:], weights.dtype),
+def fetch(weights, first, count):
+    return pl.pallas_call(
+        functools.partial(fetch_kernel, first),
+        out_shape=jax.ShapeDtypeStruct((count,) + weights.shape[2:], weights.dtype),
         in_specs=[ANY_SPEC],
         out_specs=VMEM_SPEC,
         scratch_shapes=[pltpu.SemaphoreType.DMA],
         compiler_params=pltpu.CompilerParams(vmem_limit_bytes=40 << 20),
-    )(weights)
-
-
-def product_kernel(halves, columns, weights, shifted, *refs):
+    )(pltpu.with_memory_space_constraint(weights, pltpu.HBM))
+
+
+def product_kernel(halves, columns, first_weights, other_weights, shifted, *refs):
     pieces = refs[: halves * PLANE]
     currents_hbm, future_hbm, whole, total, sems = refs[halves * PLANE :]
     step = pieces[0].shape[0] // BLK
-    row_blocks, slots = weights.shape[:2]
+    row_blocks, slots = columns.shape[1:]
+    cut = first_weights.shape[0]
     mine = lax.rem(lax.axis_index("delay"), PLANE)
     row = lax.axis_index("row")
     for turn in range(halves):
@@ -124,27 +140,21 @@
         rows = pl.ds(r * BLK, BLK)
         return pltpu.make_async_copy(total.at[rows], future_hbm.at[rows], sems.at[r])
 
-    def one_row(r, carry):
-        left = jnp.concatenate([weights[r, k] for k in range(slots)], axis=1)
+    for r in range(row_blocks):
+        weights, at = (first_weights, r) if r < cut else (other_weights, r - cut)
+        left = jnp.concatenate([weights[at, k] for k in range(slots)], axis=1)
         right = jnp.concatenate([whole[columns[0, r, k]] for k in range(slots)], axis=0)
-        rows = pl.ds(pl.multiple_of(r * BLK, BLK), BLK)
+        rows = pl.ds(r * BLK, BLK)
         added = jnp.dot(left, right, preferred_element_type=jnp.float32)
         total[rows, :] = shifted[rows, :].astype(jnp.float32) + added
         out_copy(r).start()
-        return carry
-
-    lax.fori_loop(0, row_blocks, one_row, 0)
     own.wait()
-
-    def one_wait(r, carry):
+    for r in range(row_blocks):
         out_copy(r).wait()
-        return carry
-
-    lax.fori_loop(0, row_blocks, one_wait, 0)
 
 
 def product(columns, weights, shifted, pieces, halves):
-    row_blocks = weights.shape[0]
+    row_blocks = columns.shape[1]
     rows, width = shifted.shape
     return pl.pallas_call(
         functools.partial(product_kernel, halves),
@@ -152,7 +162,7 @@
             jax.ShapeDtypeStruct((row_blocks, BLK, width), jnp.bfloat16),
             jax.ShapeDtypeStruct((rows, width), jnp.float32),
         ],
-        in_specs=[SMEM_SPEC, VMEM_SPEC, VMEM_SPEC] + [VMEM_SPEC] * len(pieces),
+        in_specs=[SMEM_SPEC] + [VMEM_SPEC] * (3 + len(pieces)),
         out_specs=[ANY_SPEC, ANY_SPEC],
         scratch_shapes=[
             pltpu.VMEM((halves * row_blocks, BLK, width), jnp.bfloat16),
@@ -160,7 +170,7 @@
             pltpu.SemaphoreType.DMA((row_blocks + 1,)),
         ],
         compiler_params=pltpu.CompilerParams(vmem_limit_bytes=40 << 20),
-    )(columns, weights, shifted, *pieces)
+    )(columns, *weights, shifted, *pieces)
 
 
 def per_device(excite, present_inverse, retarded, columns, future_in):
@@ -170,8 +180,10 @@
 
     quarters = solve(excite, present_inverse, future_in)
     spread = [lax.ppermute(quarters[k], "delay", [(0, k)]) for k in (3, 2, 1)]
-    weights, narrowed = fetch(retarded), narrow(future_in)
-    spread, weights, narrowed = lax.optimization_barrier((spread, weights, narrowed))
+    narrowed = narrow(future_in)
+    half_rows = columns.shape[1] // 2
+    first_weights = fetch(retarded, 0, half_rows)
+    spread, first_weights, narrowed = lax.optimization_barrier((spread, first_weights, narrowed))
     shifted = lax.ppermute(narrowed, "delay", [(i, i - 1) for i in range(1, delays)])
     piece = quarters[0] + spread[0] + spread[1] + spread[2]
     reach = planes
@@ -183,6 +195,8 @@
             for q in range(PLANE)
         ]
         piece = piece + lax.ppermute(piece, "delay", pairs)
+    other_weights = fetch(retarded, half_rows, half_rows)
+    piece, other_weights = lax.optimization_barrier((piece, other_weights))
     held = [piece] + [None] * (PLANE - 1)
     for mask in (3, 1, 2):
         held[mask] = lax.ppermute(piece, "delay", [(i, i ^ mask) for i in range(delays)])
@@ -190,7 +204,9 @@
     for turn in range(1, halves):
         pairs = [(i, (i + turn) % halves) for i in range(halves)]
         pieces += [lax.ppermute(p, "row", pairs) for p in held]
-    currents, future = product(columns, weights, shifted, pieces, halves)
+    currents, future = product(
+        columns, (first_weights, other_weights), shifted, pieces, halves
+    )
     return currents.reshape(1, rows, width), future[None]
 
 

time: 45.7 us -> 40.8 us (0.89)
  Pallas kernels: 14.4 us -> 11.5 us
  waiting for transfers between devices: 13.5 us -> 11.3 us
    pallas_call x1, Pallas kernels: 6.24 us -> 3.94 us  [product(): pl.pallas_call(functools.partial(product_kernel, halves), out_shape=[jax....]
    ppermute x2, waiting for transfers between devices: 3.92 us -> 1.72 us  [per_device(): piece = piece + lax.ppermute(piece, 'delay', pairs)]
    pallas_call x1, Pallas kernels: 2.68 us -> 1.89 us  [solve(): pl.pallas_call(solve_kernel, out_shape=[quarter] * PLANE, in_specs=[ANY_S...]
    pallas_call x2 -> x3, Pallas kernels: 5.53 us -> 5.64 us  [the longest x2 4.4 us: fetch(): pl.pallas_call(functools.partial(fetch_kernel, first), out_shape=jax.Shap...]
  transfers between devices with their start and end apart: 13 -> 13, of which waited for: 5 -> 5; matrix products, arithmetic and copies ran while one was open for 0% -> 0% of each run, Pallas kernels for 12% -> 14%
where the time goes in v2:
time: 40.8 us; the launch traced here: 40.2 us
  starting transfers between devices  16.6 us (41%)
  Pallas kernels  11.5 us (28%)
  waiting for transfers between devices  11.3 us (28%)
  between operations  0.78 us (2%)
    ppermute x3, waiting for transfers between devices, per_device(): lax.ppermute(piece, 'delay', [(i, i ^ mask) for i in range(delays)])  8.21 us
    ppermute x3, starting transfers between devices, per_device(): spread = [lax.ppermute(quarters[k], 'delay', [(0, k)]) for k in (3, 2, 1)]  6.65 us
    ppermute x2, starting transfers between devices, per_device(): piece = piece + lax.ppermute(piece, 'delay', pairs)  4.58 us
    pallas_call x2, Pallas kernels, fetch(): pl.pallas_call(functools.partial(fetch_kernel, first), out_shape=jax.Shap...  4.4 us
    pallas_call x1, Pallas kernels, product(): pl.pallas_call(functools.partial(product_kernel, halves), out_shape=[jax....  3.94 us
    ppermute x3, starting transfers between devices, per_device(): lax.ppermute(piece, 'delay', [(i, i ^ mask) for i in range(delays)])  3.55 us
    pallas_call x1, Pallas kernels, solve(): pl.pallas_call(solve_kernel, out_shape=[quarter] * PLANE, in_specs=[ANY_S...  1.89 us
    ppermute x2, waiting for transfers between devices, per_device(): piece = piece + lax.ppermute(piece, 'delay', pairs)  1.72 us
  transfers between devices with their start and end apart: 13, of which 5 were waited for; matrix products, arithmetic and copies ran while one was open for 0% of the time, Pallas kernels for 14%

profile of v2, /device:TPU:0, one launch (start us, length us, event | category | flops | bytes accessed | tf_op | source)
XLA Modules:
  0.0 40.2 jit_solution(6365915741445983203)
XLA Ops:
  0.6 1.9 %shard_map.68 = (bf16[512,128]{1,0:T(8,128)(2,1)S(1)}, bf16[512,128]{1,0:T(8,128)(2,1)S(1)}, bf16[512,128]{1,0:T(8,128)(2,1)S(1)}, bf16[512,128]{1,0:T(8,128)(2,1)S(1)}) custom-call(bf16[1,2048,128]{2,1,0:T(8,128)(2,1)} %excite_hbm.1, bf16[16,128,128]{2,1,0:T(8,128)(2,1)} %inverse_hbm.1, f32[1,2048,128]{2,1,0:T(8,128)} %future_hbm.3), custom_call_target="tpu_custom_call" | custom-call | tf_op jit(solution)/shard_map/pallas_call | solution.py:58
  2.5 4.1 %collective-permute-start = (bf16[512,128]{1,0:T(8,128)(2,1)S(1)}, bf16[512,128]{1,0:T(8,128)(2,1)S(1)}, u32[]{:S(2)}, u32[]{:S(2)}) collective-permute-start(bf16[512,128]{1,0:T(8,128)(2,1)S(1)} %get-tuple-element.15), channel_id=1, source_target_pairs={{0,6},{1,7}} | collective-permute-start | bytes 393224 | tf_op jit(solution)/shard_map/ppermute | solution.py:182
  6.6 1.3 %collective-permute-start.1 = (bf16[512,128]{1,0:T(8,128)(2,1)S(1)}, bf16[512,128]{1,0:T(8,128)(2,1)S(1)}, u32[]{:S(2)}, u32[]{:S(2)}) collective-permute-start(bf16[512,128]{1,0:T(8,128)(2,1)S(1)} %get-tuple-element.16), channel_id=1, source_target_pairs={{0,4},{1,5}} | collective-permute-start | bytes 393224 | tf_op jit(solution)/shard_map/ppermute | solution.py:182
  7.9 1.3 %collective-permute-start.2 = (bf16[512,128]{1,0:T(8,128)(2,1)S(1)}, bf16[512,128]{1,0:T(8,128)(2,1)S(1)}, u32[]{:S(2)}, u32[]{:S(2)}) collective-permute-start(bf16[512,128]{1,0:T(8,128)(2,1)S(1)} %get-tuple-element.17), channel_id=1, source_target_pairs={{0,2},{1,3}} | collective-permute-start | bytes 393224 | tf_op jit(solution)/shard_map/ppermute | solution.py:182
  9.2 1.2 %shard_map.70 = bf16[2048,128]{1,0:T(8,128)(2,1)S(1)} custom-call(f32[1,2048,128]{2,1,0:T(8,128)} %future_hbm.3), custom_call_target="tpu_custom_call" | custom-call | tf_op jit(solution)/shard_map/pallas_call | solution.py:89
  10.4 2.2 %shard_map.69.first_weights = bf16[8,16,128,128]{3,2,1,0:T(8,128)(2,1)S(1)} custom-call(bf16[1,16,16,128,128]{4,3,2,1,0:T(8,128)(2,1)} %weights_hbm.3), custom_call_target="tpu_custom_call" | custom-call | tf_op jit(solution)/shard_map/pallas_call | solution.py:108
  12.7 0.0 collective-permute-done
  12.7 0.0 collective-permute-done.1
  12.7 1.3 %collective-permute-start.3 = (bf16[512,128]{1,0:T(8,128)(2,1)S(1)}, bf16[512,128]{1,0:T(8,128)(2,1)S(1)}, u32[]{:S(2)}, u32[]{:S(2)}) collective-permute-start(bf16[512,128]{1,0:T(8,128)(2,1)S(1)} %add_add_fusion), channel_id=1, source_target_pairs={{0,16},{2,18},{4,20},{6,22},{1,17},{3,19},{5,21},{7,23}} | collective-permute-start | bytes 393224 | tf_op jit(solution)/shard_map/ppermute | solution.py:197
  14.0 1.3 %collective-permute-start.5 = (bf16[2048,128]{1,0:T(8,128)(2,1)S(1)}, bf16[2048,128]{1,0:T(8,128)(2,1)S(1)}, u32[]{:S(2)}, u32[]{:S(2)}) collective-permute-start(bf16[2048,128]{1,0:T(8,128)(2,1)S(1)} %shard_map.70), channel_id=1, source_target_pairs={{2,0},{4,2},{6,4},{8,6},{10,8},{12,10},{14,12},{16,14},{18,16},{20... | collective-permute-start | bytes 1572872 | tf_op jit(solution)/shard_map/ppermute | solution.py:187
  15.3 1.4 %collective-permute-done.3 = bf16[512,128]{1,0:T(8,128)(2,1)S(1)} collective-permute-done((bf16[512,128]{1,0:T(8,128)(2,1)S(1)}, bf16[512,128]{1,0:T(8,128)(2,1)S(1)}, u32[]{:S(2)}, u32[]{:S(2)}) %collective-permute-start.3) | collective-permute-done | bytes 131104 | tf_op jit(solution)/shard_map/ppermute | solution.py:197
  16.8 0.0 copy-start
  16.8 3.3 %collective-permute-start.4 = (bf16[512,128]{1,0:T(8,128)(2,1)S(1)}, bf16[512,128]{1,0:T(8,128)(2,1)S(1)}, u32[]{:S(2)}, u32[]{:S(2)}) collective-permute-start(bf16[512,128]{1,0:T(8,128)(2,1)S(1)} %add.18), channel_id=1, source_target_pairs={{0,8},{2,10},{4,12},{6,14},{16,24},{18,26},{20,28},{22,30},{1,9},{... | collective-permute-start | bytes 393224 | tf_op jit(solution)/shard_map/ppermute | solution.py:197
  20.1 2.2 %shard_map.71.other_weights = bf16[8,16,128,128]{3,2,1,0:T(8,128)(2,1)S(1)} custom-call(bf16[1,16,16,128,128]{4,3,2,1,0:T(8,128)(2,1)} %weights_hbm.3), custom_call_target="tpu_custom_call" | custom-call | tf_op jit(solution)/shard_map/pallas_call | solution.py:108
  22.3 0.3 collective-permute-done.4
  22.6 0.1 collective-permute-start.8
  22.7 1.2 %collective-permute-start.7 = (bf16[512,128]{1,0:T(8,128)(2,1)S(1)}, bf16[512,128]{1,0:T(8,128)(2,1)S(1)}, u32[]{:S(2)}, u32[]{:S(2)}) collective-permute-start(bf16[512,128]{1,0:T(8,128)(2,1)S(1)} %add.19.refs_0_), channel_id=1, source_target_pairs={{0,4},{2,6},{4,0},{6,2},{8,12},{10,14},{12,8},{14,10},{16,20},{18,... | collective-permute-start | bytes 393224 | tf_op jit(solution)/shard_map/ppermute | solution.py:202
  23.9 2.3 %collective-permute-start.6 = (bf16[512,128]{1,0:T(8,128)(2,1)S(1)}, bf16[512,128]{1,0:T(8,128)(2,1)S(1)}, u32[]{:S(2)}, u32[]{:S(2)}) collective-permute-start(bf16[512,128]{1,0:T(8,128)(2,1)S(1)} %add.19.refs_0_), channel_id=1, source_target_pairs={{0,2},{2,0},{4,6},{6,4},{8,10},{10,8},{12,14},{14,12},{16,18},{18,... | collective-permute-start | bytes 393224 | tf_op jit(solution)/shard_map/ppermute | solution.py:202
  26.2 0.0 collective-permute-start.9
  26.2 6.6 %collective-permute-done.8.refs_3_ = bf16[512,128]{1,0:T(8,128)(2,1)S(1)} collective-permute-done((bf16[512,128]{1,0:T(8,128)(2,1)S(1)}, bf16[512,128]{1,0:T(8,128)(2,1)S(1)}, u32[]{:S(2)}, u32[]{:S(2)}) %collective-permute-start.8) | collective-permute-done | bytes 131104 | tf_op jit(solution)/shard_map/ppermute | solution.py:202
  32.8 0.5 %collective-permute-start.11 = (bf16[512,128]{1,0:T(8,128)(2,1)S(1)}, bf16[512,128]{1,0:T(8,128)(2,1)S(1)}, u32[]{:S(2)}, u32[]{:S(2)}) collective-permute-start(bf16[512,128]{1,0:T(8,128)(2,1)S(1)} %collective-permute-done.7.refs_2_), channel_id=1, source_target_pairs={{0,1},{1,0},{2,3},{3,2},{4,5},{5,4},{6,7},{7,6},{8,9},{9,8},{10,11... | collective-permute-start | bytes 393224 | tf_op jit(solution)/shard_map/ppermute | solution.py:206
  33.3 1.6 %collective-permute-done.6.refs_1_ = bf16[512,128]{1,0:T(8,128)(2,1)S(1)} collective-permute-done((bf16[512,128]{1,0:T(8,128)(2,1)S(1)}, bf16[512,128]{1,0:T(8,128)(2,1)S(1)}, u32[]{:S(2)}, u32[]{:S(2)}) %collective-permute-start.6) | collective-permute-done | bytes 131104 | tf_op jit(solution)/shard_map/ppermute | solution.py:202
  34.9 1.3 %collective-permute-done.10.refs_5_ = bf16[512,128]{1,0:T(8,128)(2,1)S(1)} collective-permute-done((bf16[512,128]{1,0:T(8,128)(2,1)S(1)}, bf16[512,128]{1,0:T(8,128)(2,1)S(1)}, u32[]{:S(2)}, u32[]{:S(2)}) %collective-permute-start.10) | collective-permute-done | bytes 131104 | tf_op jit(solution)/shard_map/ppermute | solution.py:206
  36.3 3.9 %shard_map.72 = (bf16[16,128,128]{2,1,0:T(8,128)(2,1)}, f32[2048,128]{1,0:T(8,128)}) custom-call(s32[1,16,16]{2,1,0:T(8,128)S(1)} %copy-done, bf16[8,16,128,128]{3,2,1,0:T(8,128)(2,1)S(1)} %shard_map.69.first_weights, bf16[8,16,128,128]{3,2,1,0:T(8,128)(2,1)S(1)} %shard_map.71.other_weights, bf16[2048,128]{1,0:T(8,128)(2,1)S(1)} %collective-permute-done.5.shifted, ...), custom_call_target="tpu_custom_call" | custom-call | tf_op jit(solution)/shard_map/pallas_call | solution.py:159
  (12 shorter events, 0.1 us)
Async XLA Ops:
  2.5 10.1 %collective-permute-start = (bf16[512,128]{1,0:T(8,128)(2,1)S(1)}, bf16[512,128]{1,0:T(8,128)(2,1)S(1)}, u32[]{:S(2)}, u32[]{:S(2)}) collective-permute-start(bf16[512,128]{1,0:T(8,128)(2,1)S(1)} %get-tuple-element.15), channel_id=1, source_target_pairs={{0,6},{1,7}} | collective-permute-start | bytes 393224 | tf_op jit(solution)/shard_map/ppermute | solution.py:182
  6.6 6.1 %collective-permute-start.1 = (bf16[512,128]{1,0:T(8,128)(2,1)S(1)}, bf16[512,128]{1,0:T(8,128)(2,1)S(1)}, u32[]{:S(2)}, u32[]{:S(2)}) collective-permute-start(bf16[512,128]{1,0:T(8,128)(2,1)S(1)} %get-tuple-element.16), channel_id=1, source_target_pairs={{0,4},{1,5}} | collective-permute-start | bytes 393224 | tf_op jit(solution)/shard_map/ppermute | solution.py:182
  7.9 4.8 %collective-permute-start.2 = (bf16[512,128]{1,0:T(8,128)(2,1)S(1)}, bf16[512,128]{1,0:T(8,128)(2,1)S(1)}, u32[]{:S(2)}, u32[]{:S(2)}) collective-permute-start(bf16[512,128]{1,0:T(8,128)(2,1)S(1)} %get-tuple-element.17), channel_id=1, source_target_pairs={{0,2},{1,3}} | collective-permute-start | bytes 393224 | tf_op jit(solution)/shard_map/ppermute | solution.py:182
  12.7 4.0 %collective-permute-start.3 = (bf16[512,128]{1,0:T(8,128)(2,1)S(1)}, bf16[512,128]{1,0:T(8,128)(2,1)S(1)}, u32[]{:S(2)}, u32[]{:S(2)}) collective-permute-start(bf16[512,128]{1,0:T(8,128)(2,1)S(1)} %add_add_fusion), channel_id=1, source_target_pairs={{0,16},{2,18},{4,20},{6,22},{1,17},{3,19},{5,21},{7,23}} | collective-permute-start | bytes 393224 | tf_op jit(solution)/shard_map/ppermute | solution.py:197
  14.0 22.2 %collective-permute-start.5 = (bf16[2048,128]{1,0:T(8,128)(2,1)S(1)}, bf16[2048,128]{1,0:T(8,128)(2,1)S(1)}, u32[]{:S(2)}, u32[]{:S(2)}) collective-permute-start(bf16[2048,128]{1,0:T(8,128)(2,1)S(1)} %shard_map.70), channel_id=1, source_target_pairs={{2,0},{4,2},{6,4},{8,6},{10,8},{12,10},{14,12},{16,14},{18,16},{20... | collective-permute-start | bytes 1572872 | tf_op jit(solution)/shard_map/ppermute | solution.py:187
  16.8 19.5 %copy-start = (s32[1,16,16]{2,1,0:T(8,128)S(1)}, s32[1,16,16]{2,1,0:T(8,128)}, u32[]{:S(2)}) copy-start(s32[1,16,16]{2,1,0:T(8,128)} %columns.1) | copy-start | bytes 3076
  16.8 5.8 %collective-permute-start.4 = (bf16[512,128]{1,0:T(8,128)(2,1)S(1)}, bf16[512,128]{1,0:T(8,128)(2,1)S(1)}, u32[]{:S(2)}, u32[]{:S(2)}) collective-permute-start(bf16[512,128]{1,0:T(8,128)(2,1)S(1)} %add.18), channel_id=1, source_target_pairs={{0,8},{2,10},{4,12},{6,14},{16,24},{18,26},{20,28},{22,30},{1,9},{... | collective-permute-start | bytes 393224 | tf_op jit(solution)/shard_map/ppermute | solution.py:197
  22.6 10.1 %collective-permute-start.8 = (bf16[512,128]{1,0:T(8,128)(2,1)S(1)}, bf16[512,128]{1,0:T(8,128)(2,1)S(1)}, u32[]{:S(2)}, u32[]{:S(2)}) collective-permute-start(bf16[512,128]{1,0:T(8,128)(2,1)S(1)} %add.19.refs_0_), channel_id=1, source_target_pairs={{0,6},{2,4},{4,2},{6,0},{8,14},{10,12},{12,10},{14,8},{16,22},{18,... | collective-permute-start | bytes 393224 | tf_op jit(solution)/shard_map/ppermute | solution.py:202
  22.7 10.1 %collective-permute-start.7 = (bf16[512,128]{1,0:T(8,128)(2,1)S(1)}, bf16[512,128]{1,0:T(8,128)(2,1)S(1)}, u32[]{:S(2)}, u32[]{:S(2)}) collective-permute-start(bf16[512,128]{1,0:T(8,128)(2,1)S(1)} %add.19.refs_0_), channel_id=1, source_target_pairs={{0,4},{2,6},{4,0},{6,2},{8,12},{10,14},{12,8},{14,10},{16,20},{18,... | collective-permute-start | bytes 393224 | tf_op jit(solution)/shard_map/ppermute | solution.py:202
  23.9 11.1 %collective-permute-start.6 = (bf16[512,128]{1,0:T(8,128)(2,1)S(1)}, bf16[512,128]{1,0:T(8,128)(2,1)S(1)}, u32[]{:S(2)}, u32[]{:S(2)}) collective-permute-start(bf16[512,128]{1,0:T(8,128)(2,1)S(1)} %add.19.refs_0_), channel_id=1, source_target_pairs={{0,2},{2,0},{4,6},{6,4},{8,10},{10,8},{12,14},{14,12},{16,18},{18,... | collective-permute-start | bytes 393224 | tf_op jit(solution)/shard_map/ppermute | solution.py:202
  26.2 8.7 %collective-permute-start.9 = (bf16[512,128]{1,0:T(8,128)(2,1)S(1)}, bf16[512,128]{1,0:T(8,128)(2,1)S(1)}, u32[]{:S(2)}, u32[]{:S(2)}) collective-permute-start(bf16[512,128]{1,0:T(8,128)(2,1)S(1)} %add.19.refs_0_), channel_id=1, source_target_pairs={{0,1},{1,0},{2,3},{3,2},{4,5},{5,4},{6,7},{7,6},{8,9},{9,8},{10,11... | collective-permute-start | bytes 393224 | tf_op jit(solution)/shard_map/ppermute | solution.py:206
  32.8 2.1 %collective-permute-start.12 = (bf16[512,128]{1,0:T(8,128)(2,1)S(1)}, bf16[512,128]{1,0:T(8,128)(2,1)S(1)}, u32[]{:S(2)}, u32[]{:S(2)}) collective-permute-start(bf16[512,128]{1,0:T(8,128)(2,1)S(1)} %collective-permute-done.8.refs_3_), channel_id=1, source_target_pairs={{0,1},{1,0},{2,3},{3,2},{4,5},{5,4},{6,7},{7,6},{8,9},{9,8},{10,11... | collective-permute-start | bytes 393224 | tf_op jit(solution)/shard_map/ppermute | solution.py:206
  32.8 2.1 %collective-permute-start.11 = (bf16[512,128]{1,0:T(8,128)(2,1)S(1)}, bf16[512,128]{1,0:T(8,128)(2,1)S(1)}, u32[]{:S(2)}, u32[]{:S(2)}) collective-permute-start(bf16[512,128]{1,0:T(8,128)(2,1)S(1)} %collective-permute-done.7.refs_2_), channel_id=1, source_target_pairs={{0,1},{1,0},{2,3},{3,2},{4,5},{5,4},{6,7},{7,6},{8,9},{9,8},{10,11... | collective-permute-start | bytes 393224 | tf_op jit(solution)/shard_map/ppermute | solution.py:206
  34.9 1.3 %collective-permute-start.10 = (bf16[512,128]{1,0:T(8,128)(2,1)S(1)}, bf16[512,128]{1,0:T(8,128)(2,1)S(1)}, u32[]{:S(2)}, u32[]{:S(2)}) collective-permute-start(bf16[512,128]{1,0:T(8,128)(2,1)S(1)} %collective-permute-done.6.refs_1_), channel_id=1, source_target_pairs={{0,1},{1,0},{2,3},{3,2},{4,5},{5,4},{6,7},{7,6},{8,9},{9,8},{10,11... | collective-permute-start | bytes 393224 | tf_op jit(solution)/shard_map/ppermute | solution.py:206

commit v3 on v2

--- a/solution.py
+++ b/solution.py
@@ -200,6 +200,7 @@
     held = [piece] + [None] * (PLANE - 1)
     for mask in (3, 1, 2):
         held[mask] = lax.ppermute(piece, "delay", [(i, i ^ mask) for i in range(delays)])
+    held[3], shifted = lax.optimization_barrier((held[3], shifted))
     pieces = list(held)
     for turn in range(1, halves):
         pairs = [(i, (i + turn) % halves) for i in range(halves)]

time: 40.8 us -> 39.1 us (0.958)
  the two profiles are of different devices: /device:TPU:0 before, /device:TPU:3 now
where the time goes in v3:
time: 39.1 us; the launch traced here: 38.7 us
  starting transfers between devices  14.9 us (38%)
  waiting for transfers between devices  13.2 us (34%)
  Pallas kernels  9.72 us (25%)
  between operations  0.78 us (2%)
    ppermute x3, waiting for transfers between devices, per_device(): lax.ppermute(piece, 'delay', [(i, i ^ mask) for i in range(delays)])  6.19 us
    ppermute x4, starting transfers between devices, per_device(): pieces += [lax.ppermute(p, 'row', pairs) for p in held]  4.86 us
    pallas_call x2, Pallas kernels, fetch(): pl.pallas_call(functools.partial(fetch_kernel, first), out_shape=jax.Shap...  4.4 us
    ppermute x3, waiting for transfers between devices, per_device(): spread = [lax.ppermute(quarters[k], 'delay', [(0, k)]) for k in (3, 2, 1)]  4.1 us
    pallas_call x1, Pallas kernels, product(): pl.pallas_call(functools.partial(product_kernel, halves), out_shape=[jax....  3.94 us
    ppermute x3, starting transfers between devices, per_device(): lax.ppermute(piece, 'delay', [(i, i ^ mask) for i in range(delays)])  2.71 us
    ppermute x3, starting transfers between devices, per_device(): spread = [lax.ppermute(quarters[k], 'delay', [(0, k)]) for k in (3, 2, 1)]  2.63 us
    ppermute x2, starting transfers between devices, per_device(): piece = piece + lax.ppermute(piece, 'delay', pairs)  2.59 us
  transfers between devices with their start and end apart: 13, of which 4 were waited for; matrix products, arithmetic and copies ran while one was open for 0% of the time, Pallas kernels for 15%

profile of v3, /device:TPU:3, one launch (start us, length us, event | category | flops | bytes accessed | tf_op | source)
XLA Modules:
  0.0 38.7 jit_solution(3240741389655717534)
XLA Ops:
  0.6 0.1 shard_map.68
  0.8 0.7 %collective-permute-start = (bf16[512,128]{1,0:T(8,128)(2,1)S(1)}, bf16[512,128]{1,0:T(8,128)(2,1)S(1)}, u32[]{:S(2)}, u32[]{:S(2)}) collective-permute-start(bf16[512,128]{1,0:T(8,128)(2,1)S(1)} %get-tuple-element.17), channel_id=1, source_target_pairs={{0,6},{1,7}} | collective-permute-start | bytes 393224 | tf_op jit(solution)/shard_map/ppermute | solution.py:182
  1.5 0.7 %collective-permute-start.1 = (bf16[512,128]{1,0:T(8,128)(2,1)S(1)}, bf16[512,128]{1,0:T(8,128)(2,1)S(1)}, u32[]{:S(2)}, u32[]{:S(2)}) collective-permute-start(bf16[512,128]{1,0:T(8,128)(2,1)S(1)} %get-tuple-element.18), channel_id=1, source_target_pairs={{0,4},{1,5}} | collective-permute-start | bytes 393224 | tf_op jit(solution)/shard_map/ppermute | solution.py:182
  2.1 1.3 %collective-permute-start.2 = (bf16[512,128]{1,0:T(8,128)(2,1)S(1)}, bf16[512,128]{1,0:T(8,128)(2,1)S(1)}, u32[]{:S(2)}, u32[]{:S(2)}) collective-permute-start(bf16[512,128]{1,0:T(8,128)(2,1)S(1)} %get-tuple-element.19), channel_id=1, source_target_pairs={{0,2},{1,3}} | collective-permute-start | bytes 393224 | tf_op jit(solution)/shard_map/ppermute | solution.py:182
  3.4 1.2 %shard_map.70 = bf16[2048,128]{1,0:T(8,128)(2,1)S(1)} custom-call(f32[1,2048,128]{2,1,0:T(8,128)} %future_hbm.3), custom_call_target="tpu_custom_call" | custom-call | tf_op jit(solution)/shard_map/pallas_call | solution.py:89
  4.7 2.2 %shard_map.69.first_weights = bf16[8,16,128,128]{3,2,1,0:T(8,128)(2,1)S(1)} custom-call(bf16[1,16,16,128,128]{4,3,2,1,0:T(8,128)(2,1)} %weights_hbm.3), custom_call_target="tpu_custom_call" | custom-call | tf_op jit(solution)/shard_map/pallas_call | solution.py:108
  6.9 0.0 collective-permute-done
  6.9 4.1 %collective-permute-done.2 = bf16[512,128]{1,0:T(8,128)(2,1)S(1)} collective-permute-done((bf16[512,128]{1,0:T(8,128)(2,1)S(1)}, bf16[512,128]{1,0:T(8,128)(2,1)S(1)}, u32[]{:S(2)}, u32[]{:S(2)}) %collective-permute-start.2) | collective-permute-done | bytes 131104 | tf_op jit(solution)/shard_map/ppermute | solution.py:182
  11.0 2.1 %collective-permute-start.6 = (bf16[2048,128]{1,0:T(8,128)(2,1)S(1)}, bf16[2048,128]{1,0:T(8,128)(2,1)S(1)}, u32[]{:S(2)}, u32[]{:S(2)}) collective-permute-start(bf16[2048,128]{1,0:T(8,128)(2,1)S(1)} %shard_map.70), channel_id=1, source_target_pairs={{2,0},{4,2},{6,4},{8,6},{10,8},{12,10},{14,12},{16,14},{18,16},{20... | collective-permute-start | bytes 1572872 | tf_op jit(solution)/shard_map/ppermute | solution.py:187
  13.2 1.3 %collective-permute-start.3 = (bf16[512,128]{1,0:T(8,128)(2,1)S(1)}, bf16[512,128]{1,0:T(8,128)(2,1)S(1)}, u32[]{:S(2)}, u32[]{:S(2)}) collective-permute-start(bf16[512,128]{1,0:T(8,128)(2,1)S(1)} %add_add_fusion), channel_id=1, source_target_pairs={{0,16},{2,18},{4,20},{6,22},{1,17},{3,19},{5,21},{7,23}} | collective-permute-start | bytes 393224 | tf_op jit(solution)/shard_map/ppermute | solution.py:197
  14.5 1.9 %collective-permute-done.3 = bf16[512,128]{1,0:T(8,128)(2,1)S(1)} collective-permute-done((bf16[512,128]{1,0:T(8,128)(2,1)S(1)}, bf16[512,128]{1,0:T(8,128)(2,1)S(1)}, u32[]{:S(2)}, u32[]{:S(2)}) %collective-permute-start.3) | collective-permute-done | bytes 131104 | tf_op jit(solution)/shard_map/ppermute | solution.py:197
  16.4 0.0 copy-start
  16.5 1.3 %collective-permute-start.4 = (bf16[512,128]{1,0:T(8,128)(2,1)S(1)}, bf16[512,128]{1,0:T(8,128)(2,1)S(1)}, u32[]{:S(2)}, u32[]{:S(2)}) collective-permute-start(bf16[512,128]{1,0:T(8,128)(2,1)S(1)} %add.18), channel_id=1, source_target_pairs={{0,8},{2,10},{4,12},{6,14},{16,24},{18,26},{20,28},{22,30},{1,9},{... | collective-permute-start | bytes 393224 | tf_op jit(solution)/shard_map/ppermute | solution.py:197
  17.8 2.2 %shard_map.71.other_weights = bf16[8,16,128,128]{3,2,1,0:T(8,128)(2,1)S(1)} custom-call(bf16[1,16,16,128,128]{4,3,2,1,0:T(8,128)(2,1)} %weights_hbm.3), custom_call_target="tpu_custom_call" | custom-call | tf_op jit(solution)/shard_map/pallas_call | solution.py:108
  20.0 0.1 collective-permute-start.8
  20.1 2.4 %collective-permute-start.7 = (bf16[512,128]{1,0:T(8,128)(2,1)S(1)}, bf16[512,128]{1,0:T(8,128)(2,1)S(1)}, u32[]{:S(2)}, u32[]{:S(2)}) collective-permute-start(bf16[512,128]{1,0:T(8,128)(2,1)S(1)} %add.19.refs_0_), channel_id=1, source_target_pairs={{0,2},{2,0},{4,6},{6,4},{8,10},{10,8},{12,14},{14,12},{16,18},{18,... | collective-permute-start | bytes 393224 | tf_op jit(solution)/shard_map/ppermute | solution.py:202
  22.5 0.2 collective-permute-start.5
  22.7 2.9 %collective-permute-start.9 = (bf16[512,128]{1,0:T(8,128)(2,1)S(1)}, bf16[512,128]{1,0:T(8,128)(2,1)S(1)}, u32[]{:S(2)}, u32[]{:S(2)}) collective-permute-start(bf16[512,128]{1,0:T(8,128)(2,1)S(1)} %add.19.refs_0_), channel_id=1, source_target_pairs={{0,1},{1,0},{2,3},{3,2},{4,5},{5,4},{6,7},{7,6},{8,9},{9,8},{10,11... | collective-permute-start | bytes 393224 | tf_op jit(solution)/shard_map/ppermute | solution.py:207
  25.7 6.2 %collective-permute-done.8.refs_2_ = bf16[512,128]{1,0:T(8,128)(2,1)S(1)} collective-permute-done((bf16[512,128]{1,0:T(8,128)(2,1)S(1)}, bf16[512,128]{1,0:T(8,128)(2,1)S(1)}, u32[]{:S(2)}, u32[]{:S(2)}) %collective-permute-start.8) | collective-permute-done | bytes 131104 | tf_op jit(solution)/shard_map/ppermute | solution.py:202
  31.8 0.5 %collective-permute-start.11 = (bf16[512,128]{1,0:T(8,128)(2,1)S(1)}, bf16[512,128]{1,0:T(8,128)(2,1)S(1)}, u32[]{:S(2)}, u32[]{:S(2)}) collective-permute-start(bf16[512,128]{1,0:T(8,128)(2,1)S(1)} %collective-permute-done.8.refs_2_), channel_id=1, source_target_pairs={{0,1},{1,0},{2,3},{3,2},{4,5},{5,4},{6,7},{7,6},{8,9},{9,8},{10,11... | collective-permute-start | bytes 393224 | tf_op jit(solution)/shard_map/ppermute | solution.py:207
  32.3 0.0 collective-permute-start.10
  32.4 1.4 %collective-permute-start.12 = (bf16[512,128]{1,0:T(8,128)(2,1)S(1)}, bf16[512,128]{1,0:T(8,128)(2,1)S(1)}, u32[]{:S(2)}, u32[]{:S(2)}) collective-permute-start(bf16[512,128]{1,0:T(8,128)(2,1)S(1)} %collective-permute-done.5.refs_3_), channel_id=1, source_target_pairs={{0,1},{1,0},{2,3},{3,2},{4,5},{5,4},{6,7},{7,6},{8,9},{9,8},{10,11... | collective-permute-start | bytes 393224 | tf_op jit(solution)/shard_map/ppermute | solution.py:207
  33.8 1.0 %collective-permute-done.12.refs_7_ = bf16[512,128]{1,0:T(8,128)(2,1)S(1)} collective-permute-done((bf16[512,128]{1,0:T(8,128)(2,1)S(1)}, bf16[512,128]{1,0:T(8,128)(2,1)S(1)}, u32[]{:S(2)}, u32[]{:S(2)}) %collective-permute-start.12) | collective-permute-done | bytes 131104 | tf_op jit(solution)/shard_map/ppermute | solution.py:207
  34.8 3.9 %shard_map.72 = (bf16[16,128,128]{2,1,0:T(8,128)(2,1)}, f32[2048,128]{1,0:T(8,128)}) custom-call(s32[1,16,16]{2,1,0:T(8,128)S(1)} %copy-done, bf16[8,16,128,128]{3,2,1,0:T(8,128)(2,1)S(1)} %shard_map.69.first_weights, bf16[8,16,128,128]{3,2,1,0:T(8,128)(2,1)S(1)} %shard_map.71.other_weights, bf16[2048,128]{1,0:T(8,128)(2,1)S(1)} %collective-permute-done.6.shifted, ...), custom_call_target="tpu_custom_call" | custom-call | tf_op jit(solution)/shard_map/pallas_call | solution.py:159
  (12 shorter events, 0.1 us)
Async XLA Ops:
  0.8 6.1 %collective-permute-start = (bf16[512,128]{1,0:T(8,128)(2,1)S(1)}, bf16[512,128]{1,0:T(8,128)(2,1)S(1)}, u32[]{:S(2)}, u32[]{:S(2)}) collective-permute-start(bf16[512,128]{1,0:T(8,128)(2,1)S(1)} %get-tuple-element.17), channel_id=1, source_target_pairs={{0,6},{1,7}} | collective-permute-start | bytes 393224 | tf_op jit(solution)/shard_map/ppermute | solution.py:182
  1.5 5.4 %collective-permute-start.1 = (bf16[512,128]{1,0:T(8,128)(2,1)S(1)}, bf16[512,128]{1,0:T(8,128)(2,1)S(1)}, u32[]{:S(2)}, u32[]{:S(2)}) collective-permute-start(bf16[512,128]{1,0:T(8,128)(2,1)S(1)} %get-tuple-element.18), channel_id=1, source_target_pairs={{0,4},{1,5}} | collective-permute-start | bytes 393224 | tf_op jit(solution)/shard_map/ppermute | solution.py:182
  2.1 8.9 %collective-permute-start.2 = (bf16[512,128]{1,0:T(8,128)(2,1)S(1)}, bf16[512,128]{1,0:T(8,128)(2,1)S(1)}, u32[]{:S(2)}, u32[]{:S(2)}) collective-permute-start(bf16[512,128]{1,0:T(8,128)(2,1)S(1)} %get-tuple-element.19), channel_id=1, source_target_pairs={{0,2},{1,3}} | collective-permute-start | bytes 393224 | tf_op jit(solution)/shard_map/ppermute | solution.py:182
  11.0 21.4 %collective-permute-start.6 = (bf16[2048,128]{1,0:T(8,128)(2,1)S(1)}, bf16[2048,128]{1,0:T(8,128)(2,1)S(1)}, u32[]{:S(2)}, u32[]{:S(2)}) collective-permute-start(bf16[2048,128]{1,0:T(8,128)(2,1)S(1)} %shard_map.70), channel_id=1, source_target_pairs={{2,0},{4,2},{6,4},{8,6},{10,8},{12,10},{14,12},{16,14},{18,16},{20... | collective-permute-start | bytes 1572872 | tf_op jit(solution)/shard_map/ppermute | solution.py:187
  13.2 3.2 %collective-permute-start.3 = (bf16[512,128]{1,0:T(8,128)(2,1)S(1)}, bf16[512,128]{1,0:T(8,128)(2,1)S(1)}, u32[]{:S(2)}, u32[]{:S(2)}) collective-permute-start(bf16[512,128]{1,0:T(8,128)(2,1)S(1)} %add_add_fusion), channel_id=1, source_target_pairs={{0,16},{2,18},{4,20},{6,22},{1,17},{3,19},{5,21},{7,23}} | collective-permute-start | bytes 393224 | tf_op jit(solution)/shard_map/ppermute | solution.py:197
  16.4 18.3 %copy-start = (s32[1,16,16]{2,1,0:T(8,128)S(1)}, s32[1,16,16]{2,1,0:T(8,128)}, u32[]{:S(2)}) copy-start(s32[1,16,16]{2,1,0:T(8,128)} %columns.1) | copy-start | bytes 3076
  16.5 3.5 %collective-permute-start.4 = (bf16[512,128]{1,0:T(8,128)(2,1)S(1)}, bf16[512,128]{1,0:T(8,128)(2,1)S(1)}, u32[]{:S(2)}, u32[]{:S(2)}) collective-permute-start(bf16[512,128]{1,0:T(8,128)(2,1)S(1)} %add.18), channel_id=1, source_target_pairs={{0,8},{2,10},{4,12},{6,14},{16,24},{18,26},{20,28},{22,30},{1,9},{... | collective-permute-start | bytes 393224 | tf_op jit(solution)/shard_map/ppermute | solution.py:197
  20.0 11.8 %collective-permute-start.8 = (bf16[512,128]{1,0:T(8,128)(2,1)S(1)}, bf16[512,128]{1,0:T(8,128)(2,1)S(1)}, u32[]{:S(2)}, u32[]{:S(2)}) collective-permute-start(bf16[512,128]{1,0:T(8,128)(2,1)S(1)} %add.19.refs_0_), channel_id=1, source_target_pairs={{0,4},{2,6},{4,0},{6,2},{8,12},{10,14},{12,8},{14,10},{16,20},{18,... | collective-permute-start | bytes 393224 | tf_op jit(solution)/shard_map/ppermute | solution.py:202
  20.1 12.2 %collective-permute-start.7 = (bf16[512,128]{1,0:T(8,128)(2,1)S(1)}, bf16[512,128]{1,0:T(8,128)(2,1)S(1)}, u32[]{:S(2)}, u32[]{:S(2)}) collective-permute-start(bf16[512,128]{1,0:T(8,128)(2,1)S(1)} %add.19.refs_0_), channel_id=1, source_target_pairs={{0,2},{2,0},{4,6},{6,4},{8,10},{10,8},{12,14},{14,12},{16,18},{18,... | collective-permute-start | bytes 393224 | tf_op jit(solution)/shard_map/ppermute | solution.py:202
  22.5 9.8 %collective-permute-start.5 = (bf16[512,128]{1,0:T(8,128)(2,1)S(1)}, bf16[512,128]{1,0:T(8,128)(2,1)S(1)}, u32[]{:S(2)}, u32[]{:S(2)}) collective-permute-start(bf16[512,128]{1,0:T(8,128)(2,1)S(1)} %add.19.refs_0_), channel_id=1, source_target_pairs={{0,6},{2,4},{4,2},{6,0},{8,14},{10,12},{12,10},{14,8},{16,22},{18,... | collective-permute-start | bytes 393224 | tf_op jit(solution)/shard_map/ppermute | solution.py:202
  22.7 11.1 %collective-permute-start.9 = (bf16[512,128]{1,0:T(8,128)(2,1)S(1)}, bf16[512,128]{1,0:T(8,128)(2,1)S(1)}, u32[]{:S(2)}, u32[]{:S(2)}) collective-permute-start(bf16[512,128]{1,0:T(8,128)(2,1)S(1)} %add.19.refs_0_), channel_id=1, source_target_pairs={{0,1},{1,0},{2,3},{3,2},{4,5},{5,4},{6,7},{7,6},{8,9},{9,8},{10,11... | collective-permute-start | bytes 393224 | tf_op jit(solution)/shard_map/ppermute | solution.py:207
  31.8 2.0 %collective-permute-start.11 = (bf16[512,128]{1,0:T(8,128)(2,1)S(1)}, bf16[512,128]{1,0:T(8,128)(2,1)S(1)}, u32[]{:S(2)}, u32[]{:S(2)}) collective-permute-start(bf16[512,128]{1,0:T(8,128)(2,1)S(1)} %collective-permute-done.8.refs_2_), channel_id=1, source_target_pairs={{0,1},{1,0},{2,3},{3,2},{4,5},{5,4},{6,7},{7,6},{8,9},{9,8},{10,11... | collective-permute-start | bytes 393224 | tf_op jit(solution)/shard_map/ppermute | solution.py:207
  32.3 1.5 %collective-permute-start.10 = (bf16[512,128]{1,0:T(8,128)(2,1)S(1)}, bf16[512,128]{1,0:T(8,128)(2,1)S(1)}, u32[]{:S(2)}, u32[]{:S(2)}) collective-permute-start(bf16[512,128]{1,0:T(8,128)(2,1)S(1)} %collective-permute-done.7.refs_1_), channel_id=1, source_target_pairs={{0,1},{1,0},{2,3},{3,2},{4,5},{5,4},{6,7},{7,6},{8,9},{9,8},{10,11... | collective-permute-start | bytes 393224 | tf_op jit(solution)/shard_map/ppermute | solution.py:207
  32.4 2.4 %collective-permute-start.12 = (bf16[512,128]{1,0:T(8,128)(2,1)S(1)}, bf16[512,128]{1,0:T(8,128)(2,1)S(1)}, u32[]{:S(2)}, u32[]{:S(2)}) collective-permute-start(bf16[512,128]{1,0:T(8,128)(2,1)S(1)} %collective-permute-done.5.refs_3_), channel_id=1, source_target_pairs={{0,1},{1,0},{2,3},{3,2},{4,5},{5,4},{6,7},{7,6},{8,9},{9,8},{10,11... | collective-permute-start | bytes 393224 | tf_op jit(solution)/shard_map/ppermute | solution.py:207

commit v4 on v3

--- a/solution.py
+++ b/solution.py
@@ -183,7 +183,7 @@
     narrowed = narrow(future_in)
     half_rows = columns.shape[1] // 2
     first_weights = fetch(retarded, 0, half_rows)
-    spread, first_weights, narrowed = lax.optimization_barrier((spread, first_weights, narrowed))
+    spread[0], first_weights, narrowed = lax.optimization_barrier((spread[0], first_weights, narrowed))
     shifted = lax.ppermute(narrowed, "delay", [(i, i - 1) for i in range(1, delays)])
     piece = quarters[0] + spread[0] + spread[1] + spread[2]
     reach = planes

time: 39.1 us -> 38 us (0.972)
  the two profiles are of different devices: /device:TPU:3 before, /device:TPU:0 now
where the time goes in v4:
time: 38 us; the launch traced here: 37.6 us
  starting transfers between devices  15.8 us (42%)
  Pallas kernels  11.5 us (30%)
  waiting for transfers between devices  9.48 us (25%)
  between operations  0.77 us (2%)
    ppermute x3, starting transfers between devices, per_device(): spread = [lax.ppermute(quarters[k], 'delay', [(0, k)]) for k in (3, 2, 1)]  6.65 us
    ppermute x3, waiting for transfers between devices, per_device(): lax.ppermute(piece, 'delay', [(i, i ^ mask) for i in range(delays)])  5.67 us
    pallas_call x2, Pallas kernels, fetch(): pl.pallas_call(functools.partial(fetch_kernel, first), out_shape=jax.Shap...  4.4 us
    pallas_call x1, Pallas kernels, product(): pl.pallas_call(functools.partial(product_kernel, halves), out_shape=[jax....  3.94 us
    ppermute x2, starting transfers between devices, per_device(): piece = piece + lax.ppermute(piece, 'delay', pairs)  3.8 us
    ppermute x3, starting transfers between devices, per_device(): lax.ppermute(piece, 'delay', [(i, i ^ mask) for i in range(delays)])  3.55 us
    ppermute x2, waiting for transfers between devices, per_device(): piece = piece + lax.ppermute(piece, 'delay', pairs)  2.79 us
    pallas_call x1, Pallas kernels, solve(): pl.pallas_call(solve_kernel, out_shape=[quarter] * PLANE, in_specs=[ANY_S...  1.89 us
  transfers between devices with their start and end apart: 13, of which 6 were waited for; matrix products, arithmetic and copies ran while one was open for 0% of the time, Pallas kernels for 15%

profile of v4, /device:TPU:0, one launch (start us, length us, event | category | flops | bytes accessed | tf_op | source)
XLA Modules:
  0.0 37.6 jit_solution(14462801502654563832)
XLA Ops:
  0.6 1.9 %shard_map.68 = (bf16[512,128]{1,0:T(8,128)(2,1)S(1)}, bf16[512,128]{1,0:T(8,128)(2,1)S(1)}, bf16[512,128]{1,0:T(8,128)(2,1)S(1)}, bf16[512,128]{1,0:T(8,128)(2,1)S(1)}) custom-call(bf16[1,2048,128]{2,1,0:T(8,128)(2,1)} %excite_hbm.1, bf16[16,128,128]{2,1,0:T(8,128)(2,1)} %inverse_hbm.1, f32[1,2048,128]{2,1,0:T(8,128)} %future_hbm.3), custom_call_target="tpu_custom_call" | custom-call | tf_op jit(solution)/shard_map/pallas_call | solution.py:58
  2.5 4.1 %collective-permute-start = (bf16[512,128]{1,0:T(8,128)(2,1)S(1)}, bf16[512,128]{1,0:T(8,128)(2,1)S(1)}, u32[]{:S(2)}, u32[]{:S(2)}) collective-permute-start(bf16[512,128]{1,0:T(8,128)(2,1)S(1)} %get-tuple-element.15), channel_id=1, source_target_pairs={{0,6},{1,7}} | collective-permute-start | bytes 393224 | tf_op jit(solution)/shard_map/ppermute | solution.py:182
  6.6 1.3 %collective-permute-start.1 = (bf16[512,128]{1,0:T(8,128)(2,1)S(1)}, bf16[512,128]{1,0:T(8,128)(2,1)S(1)}, u32[]{:S(2)}, u32[]{:S(2)}) collective-permute-start(bf16[512,128]{1,0:T(8,128)(2,1)S(1)} %get-tuple-element.19), channel_id=1, source_target_pairs={{0,4},{1,5}} | collective-permute-start | bytes 393224 | tf_op jit(solution)/shard_map/ppermute | solution.py:182
  7.9 1.3 %collective-permute-start.2 = (bf16[512,128]{1,0:T(8,128)(2,1)S(1)}, bf16[512,128]{1,0:T(8,128)(2,1)S(1)}, u32[]{:S(2)}, u32[]{:S(2)}) collective-permute-start(bf16[512,128]{1,0:T(8,128)(2,1)S(1)} %get-tuple-element.20), channel_id=1, source_target_pairs={{0,2},{1,3}} | collective-permute-start | bytes 393224 | tf_op jit(solution)/shard_map/ppermute | solution.py:182
  9.2 1.2 %shard_map.70 = bf16[2048,128]{1,0:T(8,128)(2,1)S(1)} custom-call(f32[1,2048,128]{2,1,0:T(8,128)} %future_hbm.3), custom_call_target="tpu_custom_call" | custom-call | tf_op jit(solution)/shard_map/pallas_call | solution.py:89
  10.4 2.2 %shard_map.69.first_weights = bf16[8,16,128,128]{3,2,1,0:T(8,128)(2,1)S(1)} custom-call(bf16[1,16,16,128,128]{4,3,2,1,0:T(8,128)(2,1)} %weights_hbm.3), custom_call_target="tpu_custom_call" | custom-call | tf_op jit(solution)/shard_map/pallas_call | solution.py:108
  12.7 0.0 collective-permute-done
  12.7 1.3 %collective-permute-start.6 = (bf16[2048,128]{1,0:T(8,128)(2,1)S(1)}, bf16[2048,128]{1,0:T(8,128)(2,1)S(1)}, u32[]{:S(2)}, u32[]{:S(2)}) collective-permute-start(bf16[2048,128]{1,0:T(8,128)(2,1)S(1)} %shard_map.70), channel_id=1, source_target_pairs={{2,0},{4,2},{6,4},{8,6},{10,8},{12,10},{14,12},{16,14},{18,16},{20... | collective-permute-start | bytes 1572872 | tf_op jit(solution)/shard_map/ppermute | solution.py:187
  14.0 0.0 collective-permute-done.2
  14.0 2.5 %collective-permute-start.3 = (bf16[512,128]{1,0:T(8,128)(2,1)S(1)}, bf16[512,128]{1,0:T(8,128)(2,1)S(1)}, u32[]{:S(2)}, u32[]{:S(2)}) collective-permute-start(bf16[512,128]{1,0:T(8,128)(2,1)S(1)} %add_add_fusion), channel_id=1, source_target_pairs={{0,16},{2,18},{4,20},{6,22},{1,17},{3,19},{5,21},{7,23}} | collective-permute-start | bytes 393224 | tf_op jit(solution)/shard_map/ppermute | solution.py:197
  16.5 2.5 %collective-permute-done.3 = bf16[512,128]{1,0:T(8,128)(2,1)S(1)} collective-permute-done((bf16[512,128]{1,0:T(8,128)(2,1)S(1)}, bf16[512,128]{1,0:T(8,128)(2,1)S(1)}, u32[]{:S(2)}, u32[]{:S(2)}) %collective-permute-start.3) | collective-permute-done | bytes 131104 | tf_op jit(solution)/shard_map/ppermute | solution.py:197
  19.1 0.0 copy-start
  19.1 1.3 %collective-permute-start.4 = (bf16[512,128]{1,0:T(8,128)(2,1)S(1)}, bf16[512,128]{1,0:T(8,128)(2,1)S(1)}, u32[]{:S(2)}, u32[]{:S(2)}) collective-permute-start(bf16[512,128]{1,0:T(8,128)(2,1)S(1)} %add.18), channel_id=1, source_target_pairs={{0,8},{2,10},{4,12},{6,14},{16,24},{18,26},{20,28},{22,30},{1,9},{... | collective-permute-start | bytes 393224 | tf_op jit(solution)/shard_map/ppermute | solution.py:197
  20.4 2.2 %shard_map.71.other_weights = bf16[8,16,128,128]{3,2,1,0:T(8,128)(2,1)S(1)} custom-call(bf16[1,16,16,128,128]{4,3,2,1,0:T(8,128)(2,1)} %weights_hbm.3), custom_call_target="tpu_custom_call" | custom-call | tf_op jit(solution)/shard_map/pallas_call | solution.py:108
  22.6 0.3 collective-permute-done.4
  22.9 0.7 %collective-permute-start.8 = (bf16[512,128]{1,0:T(8,128)(2,1)S(1)}, bf16[512,128]{1,0:T(8,128)(2,1)S(1)}, u32[]{:S(2)}, u32[]{:S(2)}) collective-permute-start(bf16[512,128]{1,0:T(8,128)(2,1)S(1)} %add.19.refs_0_), channel_id=1, source_target_pairs={{0,4},{2,6},{4,0},{6,2},{8,12},{10,14},{12,8},{14,10},{16,20},{18,... | collective-permute-start | bytes 393224 | tf_op jit(solution)/shard_map/ppermute | solution.py:202
  23.6 0.9 %collective-permute-start.7 = (bf16[512,128]{1,0:T(8,128)(2,1)S(1)}, bf16[512,128]{1,0:T(8,128)(2,1)S(1)}, u32[]{:S(2)}, u32[]{:S(2)}) collective-permute-start(bf16[512,128]{1,0:T(8,128)(2,1)S(1)} %add.19.refs_0_), channel_id=1, source_target_pairs={{0,2},{2,0},{4,6},{6,4},{8,10},{10,8},{12,14},{14,12},{16,18},{18,... | collective-permute-start | bytes 393224 | tf_op jit(solution)/shard_map/ppermute | solution.py:202
  24.5 2.0 %collective-permute-start.5 = (bf16[512,128]{1,0:T(8,128)(2,1)S(1)}, bf16[512,128]{1,0:T(8,128)(2,1)S(1)}, u32[]{:S(2)}, u32[]{:S(2)}) collective-permute-start(bf16[512,128]{1,0:T(8,128)(2,1)S(1)} %add.19.refs_0_), channel_id=1, source_target_pairs={{0,6},{2,4},{4,2},{6,0},{8,14},{10,12},{12,10},{14,8},{16,22},{18,... | collective-permute-start | bytes 393224 | tf_op jit(solution)/shard_map/ppermute | solution.py:202
  26.5 2.9 %collective-permute-done.8.refs_2_ = bf16[512,128]{1,0:T(8,128)(2,1)S(1)} collective-permute-done((bf16[512,128]{1,0:T(8,128)(2,1)S(1)}, bf16[512,128]{1,0:T(8,128)(2,1)S(1)}, u32[]{:S(2)}, u32[]{:S(2)}) %collective-permute-start.8) | collective-permute-done | bytes 131104 | tf_op jit(solution)/shard_map/ppermute | solution.py:202
  29.4 2.8 %collective-permute-done.7.refs_1_ = bf16[512,128]{1,0:T(8,128)(2,1)S(1)} collective-permute-done((bf16[512,128]{1,0:T(8,128)(2,1)S(1)}, bf16[512,128]{1,0:T(8,128)(2,1)S(1)}, u32[]{:S(2)}, u32[]{:S(2)}) %collective-permute-start.7) | collective-permute-done | bytes 131104 | tf_op jit(solution)/shard_map/ppermute | solution.py:202
  32.2 0.5 %collective-permute-start.12 = (bf16[512,128]{1,0:T(8,128)(2,1)S(1)}, bf16[512,128]{1,0:T(8,128)(2,1)S(1)}, u32[]{:S(2)}, u32[]{:S(2)}) collective-permute-start(bf16[512,128]{1,0:T(8,128)(2,1)S(1)} %collective-permute-done.5.refs_3_), channel_id=1, source_target_pairs={{0,1},{1,0},{2,3},{3,2},{4,5},{5,4},{6,7},{7,6},{8,9},{9,8},{10,11... | collective-permute-start | bytes 393224 | tf_op jit(solution)/shard_map/ppermute | solution.py:207
  32.7 0.8 %collective-permute-done.10.refs_5_ = bf16[512,128]{1,0:T(8,128)(2,1)S(1)} collective-permute-done((bf16[512,128]{1,0:T(8,128)(2,1)S(1)}, bf16[512,128]{1,0:T(8,128)(2,1)S(1)}, u32[]{:S(2)}, u32[]{:S(2)}) %collective-permute-start.10) | collective-permute-done | bytes 131104 | tf_op jit(solution)/shard_map/ppermute | solution.py:207
  33.5 0.2 collective-permute-done.12.refs_7_
  33.7 3.9 %shard_map.72 = (bf16[16,128,128]{2,1,0:T(8,128)(2,1)}, f32[2048,128]{1,0:T(8,128)}) custom-call(s32[1,16,16]{2,1,0:T(8,128)S(1)} %copy-done, bf16[8,16,128,128]{3,2,1,0:T(8,128)(2,1)S(1)} %shard_map.69.first_weights, bf16[8,16,128,128]{3,2,1,0:T(8,128)(2,1)S(1)} %shard_map.71.other_weights, bf16[2048,128]{1,0:T(8,128)(2,1)S(1)} %collective-permute-done.6.shifted, ...), custom_call_target="tpu_custom_call" | custom-call | tf_op jit(solution)/shard_map/pallas_call | solution.py:159
  (12 shorter events, 0.1 us)
Async XLA Ops:
  2.5 10.1 %collective-permute-start = (bf16[512,128]{1,0:T(8,128)(2,1)S(1)}, bf16[512,128]{1,0:T(8,128)(2,1)S(1)}, u32[]{:S(2)}, u32[]{:S(2)}) collective-permute-start(bf16[512,128]{1,0:T(8,128)(2,1)S(1)} %get-tuple-element.15), channel_id=1, source_target_pairs={{0,6},{1,7}} | collective-permute-start | bytes 393224 | tf_op jit(solution)/shard_map/ppermute | solution.py:182
  6.6 7.4 %collective-permute-start.1 = (bf16[512,128]{1,0:T(8,128)(2,1)S(1)}, bf16[512,128]{1,0:T(8,128)(2,1)S(1)}, u32[]{:S(2)}, u32[]{:S(2)}) collective-permute-start(bf16[512,128]{1,0:T(8,128)(2,1)S(1)} %get-tuple-element.19), channel_id=1, source_target_pairs={{0,4},{1,5}} | collective-permute-start | bytes 393224 | tf_op jit(solution)/shard_map/ppermute | solution.py:182
  7.9 6.1 %collective-permute-start.2 = (bf16[512,128]{1,0:T(8,128)(2,1)S(1)}, bf16[512,128]{1,0:T(8,128)(2,1)S(1)}, u32[]{:S(2)}, u32[]{:S(2)}) collective-permute-start(bf16[512,128]{1,0:T(8,128)(2,1)S(1)} %get-tuple-element.20), channel_id=1, source_target_pairs={{0,2},{1,3}} | collective-permute-start | bytes 393224 | tf_op jit(solution)/shard_map/ppermute | solution.py:182
  12.7 19.5 %collective-permute-start.6 = (bf16[2048,128]{1,0:T(8,128)(2,1)S(1)}, bf16[2048,128]{1,0:T(8,128)(2,1)S(1)}, u32[]{:S(2)}, u32[]{:S(2)}) collective-permute-start(bf16[2048,128]{1,0:T(8,128)(2,1)S(1)} %shard_map.70), channel_id=1, source_target_pairs={{2,0},{4,2},{6,4},{8,6},{10,8},{12,10},{14,12},{16,14},{18,16},{20... | collective-permute-start | bytes 1572872 | tf_op jit(solution)/shard_map/ppermute | solution.py:187
  14.0 5.0 %collective-permute-start.3 = (bf16[512,128]{1,0:T(8,128)(2,1)S(1)}, bf16[512,128]{1,0:T(8,128)(2,1)S(1)}, u32[]{:S(2)}, u32[]{:S(2)}) collective-permute-start(bf16[512,128]{1,0:T(8,128)(2,1)S(1)} %add_add_fusion), channel_id=1, source_target_pairs={{0,16},{2,18},{4,20},{6,22},{1,17},{3,19},{5,21},{7,23}} | collective-permute-start | bytes 393224 | tf_op jit(solution)/shard_map/ppermute | solution.py:197
  19.1 14.6 %copy-start = (s32[1,16,16]{2,1,0:T(8,128)S(1)}, s32[1,16,16]{2,1,0:T(8,128)}, u32[]{:S(2)}) copy-start(s32[1,16,16]{2,1,0:T(8,128)} %columns.1) | copy-start | bytes 3076
  19.1 3.8 %collective-permute-start.4 = (bf16[512,128]{1,0:T(8,128)(2,1)S(1)}, bf16[512,128]{1,0:T(8,128)(2,1)S(1)}, u32[]{:S(2)}, u32[]{:S(2)}) collective-permute-start(bf16[512,128]{1,0:T(8,128)(2,1)S(1)} %add.18), channel_id=1, source_target_pairs={{0,8},{2,10},{4,12},{6,14},{16,24},{18,26},{20,28},{22,30},{1,9},{... | collective-permute-start | bytes 393224 | tf_op jit(solution)/shard_map/ppermute | solution.py:197
  22.9 6.4 %collective-permute-start.8 = (bf16[512,128]{1,0:T(8,128)(2,1)S(1)}, bf16[512,128]{1,0:T(8,128)(2,1)S(1)}, u32[]{:S(2)}, u32[]{:S(2)}) collective-permute-start(bf16[512,128]{1,0:T(8,128)(2,1)S(1)} %add.19.refs_0_), channel_id=1, source_target_pairs={{0,4},{2,6},{4,0},{6,2},{8,12},{10,14},{12,8},{14,10},{16,20},{18,... | collective-permute-start | bytes 393224 | tf_op jit(solution)/shard_map/ppermute | solution.py:202
  23.6 8.5 %collective-permute-start.7 = (bf16[512,128]{1,0:T(8,128)(2,1)S(1)}, bf16[512,128]{1,0:T(8,128)(2,1)S(1)}, u32[]{:S(2)}, u32[]{:S(2)}) collective-permute-start(bf16[512,128]{1,0:T(8,128)(2,1)S(1)} %add.19.refs_0_), channel_id=1, source_target_pairs={{0,2},{2,0},{4,6},{6,4},{8,10},{10,8},{12,14},{14,12},{16,18},{18,... | collective-permute-start | bytes 393224 | tf_op jit(solution)/shard_map/ppermute | solution.py:202
  24.5 7.7 %collective-permute-start.5 = (bf16[512,128]{1,0:T(8,128)(2,1)S(1)}, bf16[512,128]{1,0:T(8,128)(2,1)S(1)}, u32[]{:S(2)}, u32[]{:S(2)}) collective-permute-start(bf16[512,128]{1,0:T(8,128)(2,1)S(1)} %add.19.refs_0_), channel_id=1, source_target_pairs={{0,6},{2,4},{4,2},{6,0},{8,14},{10,12},{12,10},{14,8},{16,22},{18,... | collective-permute-start | bytes 393224 | tf_op jit(solution)/shard_map/ppermute | solution.py:202
  26.5 6.2 %collective-permute-start.9 = (bf16[512,128]{1,0:T(8,128)(2,1)S(1)}, bf16[512,128]{1,0:T(8,128)(2,1)S(1)}, u32[]{:S(2)}, u32[]{:S(2)}) collective-permute-start(bf16[512,128]{1,0:T(8,128)(2,1)S(1)} %add.19.refs_0_), channel_id=1, source_target_pairs={{0,1},{1,0},{2,3},{3,2},{4,5},{5,4},{6,7},{7,6},{8,9},{9,8},{10,11... | collective-permute-start | bytes 393224 | tf_op jit(solution)/shard_map/ppermute | solution.py:207
  29.4 3.3 %collective-permute-start.11 = (bf16[512,128]{1,0:T(8,128)(2,1)S(1)}, bf16[512,128]{1,0:T(8,128)(2,1)S(1)}, u32[]{:S(2)}, u32[]{:S(2)}) collective-permute-start(bf16[512,128]{1,0:T(8,128)(2,1)S(1)} %collective-permute-done.8.refs_2_), channel_id=1, source_target_pairs={{0,1},{1,0},{2,3},{3,2},{4,5},{5,4},{6,7},{7,6},{8,9},{9,8},{10,11... | collective-permute-start | bytes 393224 | tf_op jit(solution)/shard_map/ppermute | solution.py:207
  32.2 1.3 %collective-permute-start.10 = (bf16[512,128]{1,0:T(8,128)(2,1)S(1)}, bf16[512,128]{1,0:T(8,128)(2,1)S(1)}, u32[]{:S(2)}, u32[]{:S(2)}) collective-permute-start(bf16[512,128]{1,0:T(8,128)(2,1)S(1)} %collective-permute-done.7.refs_1_), channel_id=1, source_target_pairs={{0,1},{1,0},{2,3},{3,2},{4,5},{5,4},{6,7},{7,6},{8,9},{9,8},{10,11... | collective-permute-start | bytes 393224 | tf_op jit(solution)/shard_map/ppermute | solution.py:207
  32.2 1.5 %collective-permute-start.12 = (bf16[512,128]{1,0:T(8,128)(2,1)S(1)}, bf16[512,128]{1,0:T(8,128)(2,1)S(1)}, u32[]{:S(2)}, u32[]{:S(2)}) collective-permute-start(bf16[512,128]{1,0:T(8,128)(2,1)S(1)} %collective-permute-done.5.refs_3_), channel_id=1, source_target_pairs={{0,1},{1,0},{2,3},{3,2},{4,5},{5,4},{6,7},{7,6},{8,9},{9,8},{10,11... | collective-permute-start | bytes 393224 | tf_op jit(solution)/shard_map/ppermute | solution.py:207

commit v5 on v4

--- a/solution.py
+++ b/solution.py
@@ -181,8 +181,8 @@
     quarters = solve(excite, present_inverse, future_in)
     spread = [lax.ppermute(quarters[k], "delay", [(0, k)]) for k in (3, 2, 1)]
     narrowed = narrow(future_in)
-    half_rows = columns.shape[1] // 2
-    first_weights = fetch(retarded, 0, half_rows)
+    early_rows = columns.shape[1] // 4
+    first_weights = fetch(retarded, 0, early_rows)
     spread[0], first_weights, narrowed = lax.optimization_barrier((spread[0], first_weights, narrowed))
     shifted = lax.ppermute(narrowed, "delay", [(i, i - 1) for i in range(1, delays)])
     piece = quarters[0] + spread[0] + spread[1] + spread[2]
@@ -195,7 +195,7 @@
             for q in range(PLANE)
         ]
         piece = piece + lax.ppermute(piece, "delay", pairs)
-    other_weights = fetch(retarded, half_rows, half_rows)
+    other_weights = fetch(retarded, early_rows, columns.shape[1] - early_rows)
     piece, other_weights = lax.optimization_barrier((piece, other_weights))
     held = [piece] + [None] * (PLANE - 1)
     for mask in (3, 1, 2):

time: 38 us -> 37.4 us (0.984)
  waiting for transfers between devices: 9.48 us -> 8.87 us
  transfers between devices with their start and end apart: 13 -> 13, of which waited for: 6 -> 5; matrix products, arithmetic and copies ran while one was open for 0% -> 0% of each run, Pallas kernels for 15% -> 15%
where the time goes in v5:
time: 37.4 us; the launch traced here: 37 us
  starting transfers between devices  15.8 us (42%)
  Pallas kernels  11.4 us (30%)
  waiting for transfers between devices  8.87 us (24%)
  between operations  0.78 us (2%)
    ppermute x3, starting transfers between devices, per_device(): spread = [lax.ppermute(quarters[k], 'delay', [(0, k)]) for k in (3, 2, 1)]  6.65 us
    ppermute x3, waiting for transfers between devices, per_device(): lax.ppermute(piece, 'delay', [(i, i ^ mask) for i in range(delays)])  5.34 us
    pallas_call x2, Pallas kernels, fetch(): pl.pallas_call(functools.partial(fetch_kernel, first), out_shape=jax.Shap...  4.4 us
    pallas_call x1, Pallas kernels, product(): pl.pallas_call(functools.partial(product_kernel, halves), out_shape=[jax....  3.91 us
    ppermute x2, starting transfers between devices, per_device(): piece = piece + lax.ppermute(piece, 'delay', pairs)  3.8 us
    ppermute x3, starting transfers between devices, per_device(): lax.ppermute(piece, 'delay', [(i, i ^ mask) for i in range(delays)])  3.55 us
    ppermute x2, waiting for transfers between devices, per_device(): piece = piece + lax.ppermute(piece, 'delay', pairs)  2.5 us
    pallas_call x1, Pallas kernels, solve(): pl.pallas_call(solve_kernel, out_shape=[quarter] * PLANE, in_specs=[ANY_S...  1.89 us
  transfers between devices with their start and end apart: 13, of which 5 were waited for; matrix products, arithmetic and copies ran while one was open for 0% of the time, Pallas kernels for 15%

profile of v5, /device:TPU:0, one launch (start us, length us, event | category | flops | bytes accessed | tf_op | source)
XLA Modules:
  0.0 37.0 jit_solution(16951417604174537332)
XLA Ops:
  0.6 1.9 %shard_map.68 = (bf16[512,128]{1,0:T(8,128)(2,1)S(1)}, bf16[512,128]{1,0:T(8,128)(2,1)S(1)}, bf16[512,128]{1,0:T(8,128)(2,1)S(1)}, bf16[512,128]{1,0:T(8,128)(2,1)S(1)}) custom-call(bf16[1,2048,128]{2,1,0:T(8,128)(2,1)} %excite_hbm.1, bf16[16,128,128]{2,1,0:T(8,128)(2,1)} %inverse_hbm.1, f32[1,2048,128]{2,1,0:T(8,128)} %future_hbm.3), custom_call_target="tpu_custom_call" | custom-call | tf_op jit(solution)/shard_map/pallas_call | solution.py:58
  2.5 4.1 %collective-permute-start = (bf16[512,128]{1,0:T(8,128)(2,1)S(1)}, bf16[512,128]{1,0:T(8,128)(2,1)S(1)}, u32[]{:S(2)}, u32[]{:S(2)}) collective-permute-start(bf16[512,128]{1,0:T(8,128)(2,1)S(1)} %get-tuple-element.15), channel_id=1, source_target_pairs={{0,6},{1,7}} | collective-permute-start | bytes 393224 | tf_op jit(solution)/shard_map/ppermute | solution.py:182
  6.6 1.3 %collective-permute-start.1 = (bf16[512,128]{1,0:T(8,128)(2,1)S(1)}, bf16[512,128]{1,0:T(8,128)(2,1)S(1)}, u32[]{:S(2)}, u32[]{:S(2)}) collective-permute-start(bf16[512,128]{1,0:T(8,128)(2,1)S(1)} %get-tuple-element.19), channel_id=1, source_target_pairs={{0,4},{1,5}} | collective-permute-start | bytes 393224 | tf_op jit(solution)/shard_map/ppermute | solution.py:182
  7.9 1.3 %collective-permute-start.2 = (bf16[512,128]{1,0:T(8,128)(2,1)S(1)}, bf16[512,128]{1,0:T(8,128)(2,1)S(1)}, u32[]{:S(2)}, u32[]{:S(2)}) collective-permute-start(bf16[512,128]{1,0:T(8,128)(2,1)S(1)} %get-tuple-element.20), channel_id=1, source_target_pairs={{0,2},{1,3}} | collective-permute-start | bytes 393224 | tf_op jit(solution)/shard_map/ppermute | solution.py:182
  9.2 1.2 %shard_map.70 = bf16[2048,128]{1,0:T(8,128)(2,1)S(1)} custom-call(f32[1,2048,128]{2,1,0:T(8,128)} %future_hbm.3), custom_call_target="tpu_custom_call" | custom-call | tf_op jit(solution)/shard_map/pallas_call | solution.py:89
  10.4 1.6 %shard_map.69.first_weights = bf16[4,16,128,128]{3,2,1,0:T(8,128)(2,1)S(1)} custom-call(bf16[1,16,16,128,128]{4,3,2,1,0:T(8,128)(2,1)} %weights_hbm.3), custom_call_target="tpu_custom_call" | custom-call | tf_op jit(solution)/shard_map/pallas_call | solution.py:108
  12.1 1.3 %collective-permute-start.6 = (bf16[2048,128]{1,0:T(8,128)(2,1)S(1)}, bf16[2048,128]{1,0:T(8,128)(2,1)S(1)}, u32[]{:S(2)}, u32[]{:S(2)}) collective-permute-start(bf16[2048,128]{1,0:T(8,128)(2,1)S(1)} %shard_map.70), channel_id=1, source_target_pairs={{2,0},{4,2},{6,4},{8,6},{10,8},{12,10},{14,12},{16,14},{18,16},{20... | collective-permute-start | bytes 1572872 | tf_op jit(solution)/shard_map/ppermute | solution.py:187
  13.4 0.0 collective-permute-done.1
  13.4 0.0 collective-permute-done.2
  13.4 2.5 %collective-permute-start.3 = (bf16[512,128]{1,0:T(8,128)(2,1)S(1)}, bf16[512,128]{1,0:T(8,128)(2,1)S(1)}, u32[]{:S(2)}, u32[]{:S(2)}) collective-permute-start(bf16[512,128]{1,0:T(8,128)(2,1)S(1)} %add_add_fusion), channel_id=1, source_target_pairs={{0,16},{2,18},{4,20},{6,22},{1,17},{3,19},{5,21},{7,23}} | collective-permute-start | bytes 393224 | tf_op jit(solution)/shard_map/ppermute | solution.py:197
  15.9 2.5 %collective-permute-done.3 = bf16[512,128]{1,0:T(8,128)(2,1)S(1)} collective-permute-done((bf16[512,128]{1,0:T(8,128)(2,1)S(1)}, bf16[512,128]{1,0:T(8,128)(2,1)S(1)}, u32[]{:S(2)}, u32[]{:S(2)}) %collective-permute-start.3) | collective-permute-done | bytes 131104 | tf_op jit(solution)/shard_map/ppermute | solution.py:197
  18.5 0.0 copy-start
  18.5 1.3 %collective-permute-start.4 = (bf16[512,128]{1,0:T(8,128)(2,1)S(1)}, bf16[512,128]{1,0:T(8,128)(2,1)S(1)}, u32[]{:S(2)}, u32[]{:S(2)}) collective-permute-start(bf16[512,128]{1,0:T(8,128)(2,1)S(1)} %add.18), channel_id=1, source_target_pairs={{0,8},{2,10},{4,12},{6,14},{16,24},{18,26},{20,28},{22,30},{1,9},{... | collective-permute-start | bytes 393224 | tf_op jit(solution)/shard_map/ppermute | solution.py:197
  19.8 2.8 %shard_map.71.other_weights = bf16[12,16,128,128]{3,2,1,0:T(8,128)(2,1)S(1)} custom-call(bf16[1,16,16,128,128]{4,3,2,1,0:T(8,128)(2,1)} %weights_hbm.3), custom_call_target="tpu_custom_call" | custom-call | tf_op jit(solution)/shard_map/pallas_call | solution.py:108
  22.7 0.7 %collective-permute-start.8 = (bf16[512,128]{1,0:T(8,128)(2,1)S(1)}, bf16[512,128]{1,0:T(8,128)(2,1)S(1)}, u32[]{:S(2)}, u32[]{:S(2)}) collective-permute-start(bf16[512,128]{1,0:T(8,128)(2,1)S(1)} %add.19.refs_0_), channel_id=1, source_target_pairs={{0,4},{2,6},{4,0},{6,2},{8,12},{10,14},{12,8},{14,10},{16,20},{18,... | collective-permute-start | bytes 393224 | tf_op jit(solution)/shard_map/ppermute | solution.py:202
  23.3 0.9 %collective-permute-start.7 = (bf16[512,128]{1,0:T(8,128)(2,1)S(1)}, bf16[512,128]{1,0:T(8,128)(2,1)S(1)}, u32[]{:S(2)}, u32[]{:S(2)}) collective-permute-start(bf16[512,128]{1,0:T(8,128)(2,1)S(1)} %add.19.refs_0_), channel_id=1, source_target_pairs={{0,2},{2,0},{4,6},{6,4},{8,10},{10,8},{12,14},{14,12},{16,18},{18,... | collective-permute-start | bytes 393224 | tf_op jit(solution)/shard_map/ppermute | solution.py:202
  24.2 2.0 %collective-permute-start.5 = (bf16[512,128]{1,0:T(8,128)(2,1)S(1)}, bf16[512,128]{1,0:T(8,128)(2,1)S(1)}, u32[]{:S(2)}, u32[]{:S(2)}) collective-permute-start(bf16[512,128]{1,0:T(8,128)(2,1)S(1)} %add.19.refs_0_), channel_id=1, source_target_pairs={{0,6},{2,4},{4,2},{6,0},{8,14},{10,12},{12,10},{14,8},{16,22},{18,... | collective-permute-start | bytes 393224 | tf_op jit(solution)/shard_map/ppermute | solution.py:202
  26.2 0.0 collective-permute-start.9
  26.2 2.9 %collective-permute-done.8.refs_2_ = bf16[512,128]{1,0:T(8,128)(2,1)S(1)} collective-permute-done((bf16[512,128]{1,0:T(8,128)(2,1)S(1)}, bf16[512,128]{1,0:T(8,128)(2,1)S(1)}, u32[]{:S(2)}, u32[]{:S(2)}) %collective-permute-start.8) | collective-permute-done | bytes 131104 | tf_op jit(solution)/shard_map/ppermute | solution.py:202
  29.1 2.5 %collective-permute-done.7.refs_1_ = bf16[512,128]{1,0:T(8,128)(2,1)S(1)} collective-permute-done((bf16[512,128]{1,0:T(8,128)(2,1)S(1)}, bf16[512,128]{1,0:T(8,128)(2,1)S(1)}, u32[]{:S(2)}, u32[]{:S(2)}) %collective-permute-start.7) | collective-permute-done | bytes 131104 | tf_op jit(solution)/shard_map/ppermute | solution.py:202
  31.6 0.5 %collective-permute-start.12 = (bf16[512,128]{1,0:T(8,128)(2,1)S(1)}, bf16[512,128]{1,0:T(8,128)(2,1)S(1)}, u32[]{:S(2)}, u32[]{:S(2)}) collective-permute-start(bf16[512,128]{1,0:T(8,128)(2,1)S(1)} %collective-permute-done.5.refs_3_), channel_id=1, source_target_pairs={{0,1},{1,0},{2,3},{3,2},{4,5},{5,4},{6,7},{7,6},{8,9},{9,8},{10,11... | collective-permute-start | bytes 393224 | tf_op jit(solution)/shard_map/ppermute | solution.py:207
  32.1 0.8 %collective-permute-done.10.refs_5_ = bf16[512,128]{1,0:T(8,128)(2,1)S(1)} collective-permute-done((bf16[512,128]{1,0:T(8,128)(2,1)S(1)}, bf16[512,128]{1,0:T(8,128)(2,1)S(1)}, u32[]{:S(2)}, u32[]{:S(2)}) %collective-permute-start.10) | collective-permute-done | bytes 131104 | tf_op jit(solution)/shard_map/ppermute | solution.py:207
  32.9 0.2 collective-permute-done.12.refs_7_
  33.1 3.9 %shard_map.72 = (bf16[16,128,128]{2,1,0:T(8,128)(2,1)}, f32[2048,128]{1,0:T(8,128)}) custom-call(s32[1,16,16]{2,1,0:T(8,128)S(1)} %copy-done, bf16[4,16,128,128]{3,2,1,0:T(8,128)(2,1)S(1)} %shard_map.69.first_weights, bf16[12,16,128,128]{3,2,1,0:T(8,128)(2,1)S(1)} %shard_map.71.other_weights, bf16[2048,128]{1,0:T(8,128)(2,1)S(1)} %collective-permute-done.6.shifted, ...), custom_call_target="tpu_custom_call" | custom-call | tf_op jit(solution)/shard_map/pallas_call | solution.py:159
  (12 shorter events, 0.1 us)
Async XLA Ops:
  2.5 9.5 %collective-permute-start = (bf16[512,128]{1,0:T(8,128)(2,1)S(1)}, bf16[512,128]{1,0:T(8,128)(2,1)S(1)}, u32[]{:S(2)}, u32[]{:S(2)}) collective-permute-start(bf16[512,128]{1,0:T(8,128)(2,1)S(1)} %get-tuple-element.15), channel_id=1, source_target_pairs={{0,6},{1,7}} | collective-permute-start | bytes 393224 | tf_op jit(solution)/shard_map/ppermute | solution.py:182
  6.6 6.8 %collective-permute-start.1 = (bf16[512,128]{1,0:T(8,128)(2,1)S(1)}, bf16[512,128]{1,0:T(8,128)(2,1)S(1)}, u32[]{:S(2)}, u32[]{:S(2)}) collective-permute-start(bf16[512,128]{1,0:T(8,128)(2,1)S(1)} %get-tuple-element.19), channel_id=1, source_target_pairs={{0,4},{1,5}} | collective-permute-start | bytes 393224 | tf_op jit(solution)/shard_map/ppermute | solution.py:182
  7.9 5.5 %collective-permute-start.2 = (bf16[512,128]{1,0:T(8,128)(2,1)S(1)}, bf16[512,128]{1,0:T(8,128)(2,1)S(1)}, u32[]{:S(2)}, u32[]{:S(2)}) collective-permute-start(bf16[512,128]{1,0:T(8,128)(2,1)S(1)} %get-tuple-element.20), channel_id=1, source_target_pairs={{0,2},{1,3}} | collective-permute-start | bytes 393224 | tf_op jit(solution)/shard_map/ppermute | solution.py:182
  12.1 19.5 %collective-permute-start.6 = (bf16[2048,128]{1,0:T(8,128)(2,1)S(1)}, bf16[2048,128]{1,0:T(8,128)(2,1)S(1)}, u32[]{:S(2)}, u32[]{:S(2)}) collective-permute-start(bf16[2048,128]{1,0:T(8,128)(2,1)S(1)} %shard_map.70), channel_id=1, source_target_pairs={{2,0},{4,2},{6,4},{8,6},{10,8},{12,10},{14,12},{16,14},{18,16},{20... | collective-permute-start | bytes 1572872 | tf_op jit(solution)/shard_map/ppermute | solution.py:187
  13.4 5.0 %collective-permute-start.3 = (bf16[512,128]{1,0:T(8,128)(2,1)S(1)}, bf16[512,128]{1,0:T(8,128)(2,1)S(1)}, u32[]{:S(2)}, u32[]{:S(2)}) collective-permute-start(bf16[512,128]{1,0:T(8,128)(2,1)S(1)} %add_add_fusion), channel_id=1, source_target_pairs={{0,16},{2,18},{4,20},{6,22},{1,17},{3,19},{5,21},{7,23}} | collective-permute-start | bytes 393224 | tf_op jit(solution)/shard_map/ppermute | solution.py:197
  18.5 14.6 %copy-start = (s32[1,16,16]{2,1,0:T(8,128)S(1)}, s32[1,16,16]{2,1,0:T(8,128)}, u32[]{:S(2)}) copy-start(s32[1,16,16]{2,1,0:T(8,128)} %columns.1) | copy-start | bytes 3076
  18.5 4.1 %collective-permute-start.4 = (bf16[512,128]{1,0:T(8,128)(2,1)S(1)}, bf16[512,128]{1,0:T(8,128)(2,1)S(1)}, u32[]{:S(2)}, u32[]{:S(2)}) collective-permute-start(bf16[512,128]{1,0:T(8,128)(2,1)S(1)} %add.18), channel_id=1, source_target_pairs={{0,8},{2,10},{4,12},{6,14},{16,24},{18,26},{20,28},{22,30},{1,9},{... | collective-permute-start | bytes 393224 | tf_op jit(solution)/shard_map/ppermute | solution.py:197
  22.7 6.4 %collective-permute-start.8 = (bf16[512,128]{1,0:T(8,128)(2,1)S(1)}, bf16[512,128]{1,0:T(8,128)(2,1)S(1)}, u32[]{:S(2)}, u32[]{:S(2)}) collective-permute-start(bf16[512,128]{1,0:T(8,128)(2,1)S(1)} %add.19.refs_0_), channel_id=1, source_target_pairs={{0,4},{2,6},{4,0},{6,2},{8,12},{10,14},{12,8},{14,10},{16,20},{18,... | collective-permute-start | bytes 393224 | tf_op jit(solution)/shard_map/ppermute | solution.py:202
  23.3 8.2 %collective-permute-start.7 = (bf16[512,128]{1,0:T(8,128)(2,1)S(1)}, bf16[512,128]{1,0:T(8,128)(2,1)S(1)}, u32[]{:S(2)}, u32[]{:S(2)}) collective-permute-start(bf16[512,128]{1,0:T(8,128)(2,1)S(1)} %add.19.refs_0_), channel_id=1, source_target_pairs={{0,2},{2,0},{4,6},{6,4},{8,10},{10,8},{12,14},{14,12},{16,18},{18,... | collective-permute-start | bytes 393224 | tf_op jit(solution)/shard_map/ppermute | solution.py:202
  24.2 7.3 %collective-permute-start.5 = (bf16[512,128]{1,0:T(8,128)(2,1)S(1)}, bf16[512,128]{1,0:T(8,128)(2,1)S(1)}, u32[]{:S(2)}, u32[]{:S(2)}) collective-permute-start(bf16[512,128]{1,0:T(8,128)(2,1)S(1)} %add.19.refs_0_), channel_id=1, source_target_pairs={{0,6},{2,4},{4,2},{6,0},{8,14},{10,12},{12,10},{14,8},{16,22},{18,... | collective-permute-start | bytes 393224 | tf_op jit(solution)/shard_map/ppermute | solution.py:202
  26.2 5.9 %collective-permute-start.9 = (bf16[512,128]{1,0:T(8,128)(2,1)S(1)}, bf16[512,128]{1,0:T(8,128)(2,1)S(1)}, u32[]{:S(2)}, u32[]{:S(2)}) collective-permute-start(bf16[512,128]{1,0:T(8,128)(2,1)S(1)} %add.19.refs_0_), channel_id=1, source_target_pairs={{0,1},{1,0},{2,3},{3,2},{4,5},{5,4},{6,7},{7,6},{8,9},{9,8},{10,11... | collective-permute-start | bytes 393224 | tf_op jit(solution)/shard_map/ppermute | solution.py:207
  29.1 3.0 %collective-permute-start.11 = (bf16[512,128]{1,0:T(8,128)(2,1)S(1)}, bf16[512,128]{1,0:T(8,128)(2,1)S(1)}, u32[]{:S(2)}, u32[]{:S(2)}) collective-permute-start(bf16[512,128]{1,0:T(8,128)(2,1)S(1)} %collective-permute-done.8.refs_2_), channel_id=1, source_target_pairs={{0,1},{1,0},{2,3},{3,2},{4,5},{5,4},{6,7},{7,6},{8,9},{9,8},{10,11... | collective-permute-start | bytes 393224 | tf_op jit(solution)/shard_map/ppermute | solution.py:207
  31.6 1.3 %collective-permute-start.10 = (bf16[512,128]{1,0:T(8,128)(2,1)S(1)}, bf16[512,128]{1,0:T(8,128)(2,1)S(1)}, u32[]{:S(2)}, u32[]{:S(2)}) collective-permute-start(bf16[512,128]{1,0:T(8,128)(2,1)S(1)} %collective-permute-done.7.refs_1_), channel_id=1, source_target_pairs={{0,1},{1,0},{2,3},{3,2},{4,5},{5,4},{6,7},{7,6},{8,9},{9,8},{10,11... | collective-permute-start | bytes 393224 | tf_op jit(solution)/shard_map/ppermute | solution.py:207
  31.6 1.5 %collective-permute-start.12 = (bf16[512,128]{1,0:T(8,128)(2,1)S(1)}, bf16[512,128]{1,0:T(8,128)(2,1)S(1)}, u32[]{:S(2)}, u32[]{:S(2)}) collective-permute-start(bf16[512,128]{1,0:T(8,128)(2,1)S(1)} %collective-permute-done.5.refs_3_), channel_id=1, source_target_pairs={{0,1},{1,0},{2,3},{3,2},{4,5},{5,4},{6,7},{7,6},{8,9},{9,8},{10,11... | collective-permute-start | bytes 393224 | tf_op jit(solution)/shard_map/ppermute | solution.py:207

commit v6 on v5

--- a/solution.py
+++ b/solution.py
@@ -200,7 +200,7 @@
     held = [piece] + [None] * (PLANE - 1)
     for mask in (3, 1, 2):
         held[mask] = lax.ppermute(piece, "delay", [(i, i ^ mask) for i in range(delays)])
-    held[3], shifted = lax.optimization_barrier((held[3], shifted))
+    held[1], shifted = lax.optimization_barrier((held[1], shifted))
     pieces = list(held)
     for turn in range(1, halves):
         pairs = [(i, (i + turn) % halves) for i in range(halves)]

time: 37.4 us -> 38.6 us (1.032)
  waiting for transfers between devices: 8.87 us -> 10.6 us
  starting transfers between devices: 15.8 us -> 15.3 us
    ppermute x3, waiting for transfers between devices: 5.34 us -> 6.74 us  [per_device(): lax.ppermute(piece, 'delay', [(i, i ^ mask) for i in range(delays)])]
    ppermute x4, starting transfers between devices: 0.51 us -> 0.01 us  [per_device(): pieces += [lax.ppermute(p, 'row', pairs) for p in held]]
where the time goes in v6:
time: 38.6 us; the launch traced here: 38.2 us
  starting transfers between devices  15.3 us (40%)
  Pallas kernels  11.4 us (30%)
  waiting for transfers between devices  10.6 us (27%)
  between operations  0.79 us (2%)
    ppermute x3, waiting for transfers between devices, per_device(): lax.ppermute(piece, 'delay', [(i, i ^ mask) for i in range(delays)])  6.74 us
    ppermute x3, starting transfers between devices, per_device(): spread = [lax.ppermute(quarters[k], 'delay', [(0, k)]) for k in (3, 2, 1)]  6.65 us
    pallas_call x2, Pallas kernels, fetch(): pl.pallas_call(functools.partial(fetch_kernel, first), out_shape=jax.Shap...  4.4 us
    pallas_call x1, Pallas kernels, product(): pl.pallas_call(functools.partial(product_kernel, halves), out_shape=[jax....  3.91 us
    ppermute x2, starting transfers between devices, per_device(): piece = piece + lax.ppermute(piece, 'delay', pairs)  3.8 us
    ppermute x3, starting transfers between devices, per_device(): lax.ppermute(piece, 'delay', [(i, i ^ mask) for i in range(delays)])  3.55 us
    ppermute x2, waiting for transfers between devices, per_device(): piece = piece + lax.ppermute(piece, 'delay', pairs)  2.5 us
    pallas_call x1, Pallas kernels, solve(): pl.pallas_call(solve_kernel, out_shape=[quarter] * PLANE, in_specs=[ANY_S...  1.89 us
  transfers between devices with their start and end apart: 13, of which 5 were waited for; matrix products, arithmetic and copies ran while one was open for 0% of the time, Pallas kernels for 15%

profile of v6, /device:TPU:0, one launch (start us, length us, event | category | flops | bytes accessed | tf_op | source)
XLA Modules:
  0.0 38.2 jit_solution(1656838262671945457)
XLA Ops:
  0.6 1.9 %shard_map.68 = (bf16[512,128]{1,0:T(8,128)(2,1)S(1)}, bf16[512,128]{1,0:T(8,128)(2,1)S(1)}, bf16[512,128]{1,0:T(8,128)(2,1)S(1)}, bf16[512,128]{1,0:T(8,128)(2,1)S(1)}) custom-call(bf16[1,2048,128]{2,1,0:T(8,128)(2,1)} %excite_hbm.1, bf16[16,128,128]{2,1,0:T(8,128)(2,1)} %inverse_hbm.1, f32[1,2048,128]{2,1,0:T(8,128)} %future_hbm.3), custom_call_target="tpu_custom_call" | custom-call | tf_op jit(solution)/shard_map/pallas_call | solution.py:58
  2.5 4.1 %collective-permute-start = (bf16[512,128]{1,0:T(8,128)(2,1)S(1)}, bf16[512,128]{1,0:T(8,128)(2,1)S(1)}, u32[]{:S(2)}, u32[]{:S(2)}) collective-permute-start(bf16[512,128]{1,0:T(8,128)(2,1)S(1)} %get-tuple-element.15), channel_id=1, source_target_pairs={{0,6},{1,7}} | collective-permute-start | bytes 393224 | tf_op jit(solution)/shard_map/ppermute | solution.py:182
  6.6 1.3 %collective-permute-start.1 = (bf16[512,128]{1,0:T(8,128)(2,1)S(1)}, bf16[512,128]{1,0:T(8,128)(2,1)S(1)}, u32[]{:S(2)}, u32[]{:S(2)}) collective-permute-start(bf16[512,128]{1,0:T(8,128)(2,1)S(1)} %get-tuple-element.19), channel_id=1, source_target_pairs={{0,4},{1,5}} | collective-permute-start | bytes 393224 | tf_op jit(solution)/shard_map/ppermute | solution.py:182
  7.9 1.3 %collective-permute-start.2 = (bf16[512,128]{1,0:T(8,128)(2,1)S(1)}, bf16[512,128]{1,0:T(8,128)(2,1)S(1)}, u32[]{:S(2)}, u32[]{:S(2)}) collective-permute-start(bf16[512,128]{1,0:T(8,128)(2,1)S(1)} %get-tuple-element.20), channel_id=1, source_target_pairs={{0,2},{1,3}} | collective-permute-start | bytes 393224 | tf_op jit(solution)/shard_map/ppermute | solution.py:182
  9.2 1.2 %shard_map.70 = bf16[2048,128]{1,0:T(8,128)(2,1)S(1)} custom-call(f32[1,2048,128]{2,1,0:T(8,128)} %future_hbm.3), custom_call_target="tpu_custom_call" | custom-call | tf_op jit(solution)/shard_map/pallas_call | solution.py:89
  10.4 1.6 %shard_map.69.first_weights = bf16[4,16,128,128]{3,2,1,0:T(8,128)(2,1)S(1)} custom-call(bf16[1,16,16,128,128]{4,3,2,1,0:T(8,128)(2,1)} %weights_hbm.3), custom_call_target="tpu_custom_call" | custom-call | tf_op jit(solution)/shard_map/pallas_call | solution.py:108
  12.1 0.0 collective-permute-done
  12.1 1.3 %collective-permute-start.6 = (bf16[2048,128]{1,0:T(8,128)(2,1)S(1)}, bf16[2048,128]{1,0:T(8,128)(2,1)S(1)}, u32[]{:S(2)}, u32[]{:S(2)}) collective-permute-start(bf16[2048,128]{1,0:T(8,128)(2,1)S(1)} %shard_map.70), channel_id=1, source_target_pairs={{2,0},{4,2},{6,4},{8,6},{10,8},{12,10},{14,12},{16,14},{18,16},{20... | collective-permute-start | bytes 1572872 | tf_op jit(solution)/shard_map/ppermute | solution.py:187
  13.4 0.0 collective-permute-done.2
  13.4 2.5 %collective-permute-start.3 = (bf16[512,128]{1,0:T(8,128)(2,1)S(1)}, bf16[512,128]{1,0:T(8,128)(2,1)S(1)}, u32[]{:S(2)}, u32[]{:S(2)}) collective-permute-start(bf16[512,128]{1,0:T(8,128)(2,1)S(1)} %add_add_fusion), channel_id=1, source_target_pairs={{0,16},{2,18},{4,20},{6,22},{1,17},{3,19},{5,21},{7,23}} | collective-permute-start | bytes 393224 | tf_op jit(solution)/shard_map/ppermute | solution.py:197
  15.9 2.5 %collective-permute-done.3 = bf16[512,128]{1,0:T(8,128)(2,1)S(1)} collective-permute-done((bf16[512,128]{1,0:T(8,128)(2,1)S(1)}, bf16[512,128]{1,0:T(8,128)(2,1)S(1)}, u32[]{:S(2)}, u32[]{:S(2)}) %collective-permute-start.3) | collective-permute-done | bytes 131104 | tf_op jit(solution)/shard_map/ppermute | solution.py:197
  18.5 0.0 copy-start
  18.5 1.3 %collective-permute-start.4 = (bf16[512,128]{1,0:T(8,128)(2,1)S(1)}, bf16[512,128]{1,0:T(8,128)(2,1)S(1)}, u32[]{:S(2)}, u32[]{:S(2)}) collective-permute-start(bf16[512,128]{1,0:T(8,128)(2,1)S(1)} %add.18), channel_id=1, source_target_pairs={{0,8},{2,10},{4,12},{6,14},{16,24},{18,26},{20,28},{22,30},{1,9},{... | collective-permute-start | bytes 393224 | tf_op jit(solution)/shard_map/ppermute | solution.py:197
  19.8 2.8 %shard_map.71.other_weights = bf16[12,16,128,128]{3,2,1,0:T(8,128)(2,1)S(1)} custom-call(bf16[1,16,16,128,128]{4,3,2,1,0:T(8,128)(2,1)} %weights_hbm.3), custom_call_target="tpu_custom_call" | custom-call | tf_op jit(solution)/shard_map/pallas_call | solution.py:108
  22.6 0.0 collective-permute-done.4
  22.7 0.7 %collective-permute-start.8 = (bf16[512,128]{1,0:T(8,128)(2,1)S(1)}, bf16[512,128]{1,0:T(8,128)(2,1)S(1)}, u32[]{:S(2)}, u32[]{:S(2)}) collective-permute-start(bf16[512,128]{1,0:T(8,128)(2,1)S(1)} %add.19.refs_0_), channel_id=1, source_target_pairs={{0,6},{2,4},{4,2},{6,0},{8,14},{10,12},{12,10},{14,8},{16,22},{18,... | collective-permute-start | bytes 393224 | tf_op jit(solution)/shard_map/ppermute | solution.py:202
  23.4 2.2 %collective-permute-start.7 = (bf16[512,128]{1,0:T(8,128)(2,1)S(1)}, bf16[512,128]{1,0:T(8,128)(2,1)S(1)}, u32[]{:S(2)}, u32[]{:S(2)}) collective-permute-start(bf16[512,128]{1,0:T(8,128)(2,1)S(1)} %add.19.refs_0_), channel_id=1, source_target_pairs={{0,4},{2,6},{4,0},{6,2},{8,12},{10,14},{12,8},{14,10},{16,20},{18,... | collective-permute-start | bytes 393224 | tf_op jit(solution)/shard_map/ppermute | solution.py:202
  25.6 0.6 %collective-permute-start.5 = (bf16[512,128]{1,0:T(8,128)(2,1)S(1)}, bf16[512,128]{1,0:T(8,128)(2,1)S(1)}, u32[]{:S(2)}, u32[]{:S(2)}) collective-permute-start(bf16[512,128]{1,0:T(8,128)(2,1)S(1)} %add.19.refs_0_), channel_id=1, source_target_pairs={{0,2},{2,0},{4,6},{6,4},{8,10},{10,8},{12,14},{14,12},{16,18},{18,... | collective-permute-start | bytes 393224 | tf_op jit(solution)/shard_map/ppermute | solution.py:202
  26.2 0.0 collective-permute-start.9
  26.2 3.7 %collective-permute-done.8.refs_3_ = bf16[512,128]{1,0:T(8,128)(2,1)S(1)} collective-permute-done((bf16[512,128]{1,0:T(8,128)(2,1)S(1)}, bf16[512,128]{1,0:T(8,128)(2,1)S(1)}, u32[]{:S(2)}, u32[]{:S(2)}) %collective-permute-start.8) | collective-permute-done | bytes 131104 | tf_op jit(solution)/shard_map/ppermute | solution.py:202
  29.9 0.6 %collective-permute-done.7.refs_2_ = bf16[512,128]{1,0:T(8,128)(2,1)S(1)} collective-permute-done((bf16[512,128]{1,0:T(8,128)(2,1)S(1)}, bf16[512,128]{1,0:T(8,128)(2,1)S(1)}, u32[]{:S(2)}, u32[]{:S(2)}) %collective-permute-start.7) | collective-permute-done | bytes 131104 | tf_op jit(solution)/shard_map/ppermute | solution.py:202
  30.5 2.5 %collective-permute-done.5.refs_1_ = bf16[512,128]{1,0:T(8,128)(2,1)S(1)} collective-permute-done((bf16[512,128]{1,0:T(8,128)(2,1)S(1)}, bf16[512,128]{1,0:T(8,128)(2,1)S(1)}, u32[]{:S(2)}, u32[]{:S(2)}) %collective-permute-start.5) | collective-permute-done | bytes 131104 | tf_op jit(solution)/shard_map/ppermute | solution.py:202
  33.0 1.3 %collective-permute-done.10.refs_5_ = bf16[512,128]{1,0:T(8,128)(2,1)S(1)} collective-permute-done((bf16[512,128]{1,0:T(8,128)(2,1)S(1)}, bf16[512,128]{1,0:T(8,128)(2,1)S(1)}, u32[]{:S(2)}, u32[]{:S(2)}) %collective-permute-start.10) | collective-permute-done | bytes 131104 | tf_op jit(solution)/shard_map/ppermute | solution.py:207
  34.3 3.9 %shard_map.72 = (bf16[16,128,128]{2,1,0:T(8,128)(2,1)}, f32[2048,128]{1,0:T(8,128)}) custom-call(s32[1,16,16]{2,1,0:T(8,128)S(1)} %copy-done, bf16[4,16,128,128]{3,2,1,0:T(8,128)(2,1)S(1)} %shard_map.69.first_weights, bf16[12,16,128,128]{3,2,1,0:T(8,128)(2,1)S(1)} %shard_map.71.other_weights, bf16[2048,128]{1,0:T(8,128)(2,1)S(1)} %collective-permute-done.6.shifted, ...), custom_call_target="tpu_custom_call" | custom-call | tf_op jit(solution)/shard_map/pallas_call | solution.py:159
  (12 shorter events, 0.1 us)
Async XLA Ops:
  2.5 9.5 %collective-permute-start = (bf16[512,128]{1,0:T(8,128)(2,1)S(1)}, bf16[512,128]{1,0:T(8,128)(2,1)S(1)}, u32[]{:S(2)}, u32[]{:S(2)}) collective-permute-start(bf16[512,128]{1,0:T(8,128)(2,1)S(1)} %get-tuple-element.15), channel_id=1, source_target_pairs={{0,6},{1,7}} | collective-permute-start | bytes 393224 | tf_op jit(solution)/shard_map/ppermute | solution.py:182
  6.6 6.8 %collective-permute-start.1 = (bf16[512,128]{1,0:T(8,128)(2,1)S(1)}, bf16[512,128]{1,0:T(8,128)(2,1)S(1)}, u32[]{:S(2)}, u32[]{:S(2)}) collective-permute-start(bf16[512,128]{1,0:T(8,128)(2,1)S(1)} %get-tuple-element.19), channel_id=1, source_target_pairs={{0,4},{1,5}} | collective-permute-start | bytes 393224 | tf_op jit(solution)/shard_map/ppermute | solution.py:182
  7.9 5.5 %collective-permute-start.2 = (bf16[512,128]{1,0:T(8,128)(2,1)S(1)}, bf16[512,128]{1,0:T(8,128)(2,1)S(1)}, u32[]{:S(2)}, u32[]{:S(2)}) collective-permute-start(bf16[512,128]{1,0:T(8,128)(2,1)S(1)} %get-tuple-element.20), channel_id=1, source_target_pairs={{0,2},{1,3}} | collective-permute-start | bytes 393224 | tf_op jit(solution)/shard_map/ppermute | solution.py:182
  12.1 20.9 %collective-permute-start.6 = (bf16[2048,128]{1,0:T(8,128)(2,1)S(1)}, bf16[2048,128]{1,0:T(8,128)(2,1)S(1)}, u32[]{:S(2)}, u32[]{:S(2)}) collective-permute-start(bf16[2048,128]{1,0:T(8,128)(2,1)S(1)} %shard_map.70), channel_id=1, source_target_pairs={{2,0},{4,2},{6,4},{8,6},{10,8},{12,10},{14,12},{16,14},{18,16},{20... | collective-permute-start | bytes 1572872 | tf_op jit(solution)/shard_map/ppermute | solution.py:187
  13.4 5.0 %collective-permute-start.3 = (bf16[512,128]{1,0:T(8,128)(2,1)S(1)}, bf16[512,128]{1,0:T(8,128)(2,1)S(1)}, u32[]{:S(2)}, u32[]{:S(2)}) collective-permute-start(bf16[512,128]{1,0:T(8,128)(2,1)S(1)} %add_add_fusion), channel_id=1, source_target_pairs={{0,16},{2,18},{4,20},{6,22},{1,17},{3,19},{5,21},{7,23}} | collective-permute-start | bytes 393224 | tf_op jit(solution)/shard_map/ppermute | solution.py:197
  18.5 15.8 %copy-start = (s32[1,16,16]{2,1,0:T(8,128)S(1)}, s32[1,16,16]{2,1,0:T(8,128)}, u32[]{:S(2)}) copy-start(s32[1,16,16]{2,1,0:T(8,128)} %columns.1) | copy-start | bytes 3076
  18.5 4.1 %collective-permute-start.4 = (bf16[512,128]{1,0:T(8,128)(2,1)S(1)}, bf16[512,128]{1,0:T(8,128)(2,1)S(1)}, u32[]{:S(2)}, u32[]{:S(2)}) collective-permute-start(bf16[512,128]{1,0:T(8,128)(2,1)S(1)} %add.18), channel_id=1, source_target_pairs={{0,8},{2,10},{4,12},{6,14},{16,24},{18,26},{20,28},{22,30},{1,9},{... | collective-permute-start | bytes 393224 | tf_op jit(solution)/shard_map/ppermute | solution.py:197
  22.7 7.2 %collective-permute-start.8 = (bf16[512,128]{1,0:T(8,128)(2,1)S(1)}, bf16[512,128]{1,0:T(8,128)(2,1)S(1)}, u32[]{:S(2)}, u32[]{:S(2)}) collective-permute-start(bf16[512,128]{1,0:T(8,128)(2,1)S(1)} %add.19.refs_0_), channel_id=1, source_target_pairs={{0,6},{2,4},{4,2},{6,0},{8,14},{10,12},{12,10},{14,8},{16,22},{18,... | collective-permute-start | bytes 393224 | tf_op jit(solution)/shard_map/ppermute | solution.py:202
  23.4 7.1 %collective-permute-start.7 = (bf16[512,128]{1,0:T(8,128)(2,1)S(1)}, bf16[512,128]{1,0:T(8,128)(2,1)S(1)}, u32[]{:S(2)}, u32[]{:S(2)}) collective-permute-start(bf16[512,128]{1,0:T(8,128)(2,1)S(1)} %add.19.refs_0_), channel_id=1, source_target_pairs={{0,4},{2,6},{4,0},{6,2},{8,12},{10,14},{12,8},{14,10},{16,20},{18,... | collective-permute-start | bytes 393224 | tf_op jit(solution)/shard_map/ppermute | solution.py:202
  25.6 7.3 %collective-permute-start.5 = (bf16[512,128]{1,0:T(8,128)(2,1)S(1)}, bf16[512,128]{1,0:T(8,128)(2,1)S(1)}, u32[]{:S(2)}, u32[]{:S(2)}) collective-permute-start(bf16[512,128]{1,0:T(8,128)(2,1)S(1)} %add.19.refs_0_), channel_id=1, source_target_pairs={{0,2},{2,0},{4,6},{6,4},{8,10},{10,8},{12,14},{14,12},{16,18},{18,... | collective-permute-start | bytes 393224 | tf_op jit(solution)/shard_map/ppermute | solution.py:202
  26.2 6.8 %collective-permute-start.9 = (bf16[512,128]{1,0:T(8,128)(2,1)S(1)}, bf16[512,128]{1,0:T(8,128)(2,1)S(1)}, u32[]{:S(2)}, u32[]{:S(2)}) collective-permute-start(bf16[512,128]{1,0:T(8,128)(2,1)S(1)} %add.19.refs_0_), channel_id=1, source_target_pairs={{0,1},{1,0},{2,3},{3,2},{4,5},{5,4},{6,7},{7,6},{8,9},{9,8},{10,11... | collective-permute-start | bytes 393224 | tf_op jit(solution)/shard_map/ppermute | solution.py:207
  29.9 3.1 %collective-permute-start.12 = (bf16[512,128]{1,0:T(8,128)(2,1)S(1)}, bf16[512,128]{1,0:T(8,128)(2,1)S(1)}, u32[]{:S(2)}, u32[]{:S(2)}) collective-permute-start(bf16[512,128]{1,0:T(8,128)(2,1)S(1)} %collective-permute-done.8.refs_3_), channel_id=1, source_target_pairs={{0,1},{1,0},{2,3},{3,2},{4,5},{5,4},{6,7},{7,6},{8,9},{9,8},{10,11... | collective-permute-start | bytes 393224 | tf_op jit(solution)/shard_map/ppermute | solution.py:207
  30.5 2.5 %collective-permute-start.11 = (bf16[512,128]{1,0:T(8,128)(2,1)S(1)}, bf16[512,128]{1,0:T(8,128)(2,1)S(1)}, u32[]{:S(2)}, u32[]{:S(2)}) collective-permute-start(bf16[512,128]{1,0:T(8,128)(2,1)S(1)} %collective-permute-done.7.refs_2_), channel_id=1, source_target_pairs={{0,1},{1,0},{2,3},{3,2},{4,5},{5,4},{6,7},{7,6},{8,9},{9,8},{10,11... | collective-permute-start | bytes 393224 | tf_op jit(solution)/shard_map/ppermute | solution.py:207
  33.0 1.3 %collective-permute-start.10 = (bf16[512,128]{1,0:T(8,128)(2,1)S(1)}, bf16[512,128]{1,0:T(8,128)(2,1)S(1)}, u32[]{:S(2)}, u32[]{:S(2)}) collective-permute-start(bf16[512,128]{1,0:T(8,128)(2,1)S(1)} %collective-permute-done.5.refs_1_), channel_id=1, source_target_pairs={{0,1},{1,0},{2,3},{3,2},{4,5},{5,4},{6,7},{7,6},{8,9},{9,8},{10,11... | collective-permute-start | bytes 393224 | tf_op jit(solution)/shard_map/ppermute | solution.py:207
